TPU v7x, 256 devices: a whole 4x4x8 slice. The times are simulated.
256 devices in a mesh: patch: 64 (over z, y, core), band: 4 (over x).
Axes of the slice: x: 4, y: 4, z: 8, core: 2. Of those that a mesh axis runs over, the one named last changes fastest.
Arguments:
- exposures: float32 [512, 256, 128], P(('band', 'patch')), parts along dimension 0, may hold values from -6 to 6
- variance: float32 [512, 256, 128], P(('band', 'patch')), parts along dimension 0, may hold values from 0.01 to 60, as said below
- mask_bits: int32 [512, 256, 128], P(('band', 'patch')), parts along dimension 0, may hold values from 0 to 4095
- kernel_coeffs: float32 [512, 27, 6], P(('band', 'patch')), parts along dimension 0, may hold values from -3 to 3
- ccd_visit: int32 [512, 1], P(('band', 'patch')), parts along dimension 0, may hold values from 0 to 7
- strip_patch: int32 [16384, 1], P(('band', 'patch')), parts along dimension 0, may hold values from 0 to 63, as said below
- strip_row: int32 [16384], P(('band', 'patch')), parts along dimension 0, may hold values from 0 to 120
- strip_col: int32 [16384], P(('band', 'patch')), parts along dimension 0, may hold values from 0 to 384
Outputs:
- coadd_image: float32 [256, 128, 512], P(('band', 'patch')), parts along dimension 0
- weight_map: float32 [256, 128, 512], P(('band', 'patch')), parts along dimension 0
There are 4 independent parts, one for each index of `band`. A program takes and returns all parts, laid end to end along the dimension named above; each array names one. Nothing has to cross between parts.
Inputs may be any that keep to these rules, and one draw needn't show every extreme that they name: `variance`: Positive. `ccd_visit`: every visit has at least one CCD. `strip_patch`: among the strips of one device (aligned blocks of 64 rows) no patch is named more than 2 times; one patch is named exactly 2 times in every block.
All inputs are finite; a program needn't handle non-finite values.
Results may differ from a plain program's by a relative error of at most 0.00011.
Values sent between devices are 32-bit elements; how exact they have to be, the bound alone decides.
A program may use at most 64 MiB of HBM per device.

v0:
```python
import math

import jax
import jax.numpy as jnp
from jax import lax
from jax.sharding import PartitionSpec as P

PH = 128
PW = 512
KS = 21
VISITS = 8


gauss_widths = (0.75, 1.5, 3.0)
largest_value = lax.Precision.HIGHEST


def tap_values(offsets, kernel_half_width):
    support = jnp.arange(-kernel_half_width, kernel_half_width + 1).astype(jnp.float32)
    inside = (jnp.abs(offsets) <= kernel_half_width).astype(jnp.float32)
    tables = []
    for spread in gauss_widths:
        gauss_total = jnp.sum(jnp.exp(-support * support / (2.0 * spread * spread)))
        profile = jnp.exp(-offsets * offsets / (2.0 * spread * spread)) / gauss_total * inside
        scaled = offsets / spread
        tables.append(jnp.stack([profile, profile * scaled, profile * scaled * scaled]))
    return jnp.stack(tables)


def row_filters(row_count, kernel_half_width):
    row_ids = jnp.arange(row_count)[:, None]
    window_ids = jnp.arange(row_count + 2 * kernel_half_width)[None, :]
    return tap_values(
        (window_ids - row_ids - kernel_half_width).astype(jnp.float32), kernel_half_width
    )


def column_filters(column_count, kernel_half_width):
    source = jnp.arange(column_count)[:, None]
    target_patch = jnp.arange(column_count)[None, :]
    return tap_values((source - target_patch).astype(jnp.float32), kernel_half_width)


def convolve(windows, kernel_terms, height):
    kernel_half_width = KS // 2
    batch_size = windows.shape[0]
    row_count = windows.shape[1] - 2 * kernel_half_width
    columns = windows.shape[2]
    smooth = jnp.einsum(
        "gaij,njc->ngaic",
        row_filters(row_count, kernel_half_width),
        windows,
        precision=largest_value,
    )
    column_ops = column_filters(columns, kernel_half_width)
    row_coords = jnp.arange(row_count).astype(jnp.float32)[None, :]
    y_plane = jnp.broadcast_to(
        (2.0 * row_coords / (height - 1) - 1.0)[:, :, None], (batch_size, row_count, columns)
    )
    x_line = 2.0 * jnp.arange(columns).astype(jnp.float32) / (columns - 1) - 1.0
    x_plane = jnp.broadcast_to(x_line[None, None, :], (batch_size, row_count, columns))
    ones_plane = jnp.ones((batch_size, row_count, columns), jnp.float32)
    poly_planes = jnp.stack(
        [ones_plane, x_plane, y_plane, x_plane * x_plane, x_plane * y_plane, y_plane * y_plane],
        axis=1,
    )
    kernel_split = kernel_terms.reshape(batch_size, 3, 9, kernel_terms.shape[2])
    result = jnp.zeros((batch_size, row_count, columns), jnp.float32)
    for gauss_index in range(3):
        basis_images = jnp.einsum(
            "naic,bcd->nabid",
            smooth[:, gauss_index],
            column_ops[gauss_index],
            precision=largest_value,
        )
        fields = jnp.einsum(
            "nkp,npid->nkid", kernel_split[:, gauss_index], poly_planes, precision=largest_value
        )
        fields = fields.reshape(batch_size, 3, 3, row_count, columns)
        result = result + jnp.sum(basis_images * fields, axis=(1, 2))
    return result


def place_slots(flux_flat, weight_flat, offsets, patch_rows, patch_cols):
    slot_total, strip_rows, columns = flux_flat.shape
    group = math.gcd(slot_total, 16)
    pairs = jnp.stack([flux_flat, weight_flat], axis=1).reshape(
        slot_total // group, group, 2, strip_rows, columns
    )
    grouped_offsets = offsets.reshape(slot_total // group, group, offsets.shape[1])
    target_cols = jnp.arange(patch_cols)
    source_cols = jnp.arange(columns)
    target_rows = jnp.arange(patch_rows)
    source_rows = jnp.arange(strip_rows)

    def place_group(total, item):
        pixel_block_tile, block_offsets = item
        column_selection = (
            target_cols[None, None, :]
            == block_offsets[:, 1][:, None, None] + source_cols[None, :, None]
        ).astype(jnp.float32)
        row_select = (
            target_rows[None, :, None]
            == block_offsets[:, 0][:, None, None] + source_rows[None, None, :]
        ).astype(jnp.float32)
        broadened_width = jnp.einsum(
            "vmwn,vny->vmwy", pixel_block_tile, column_selection, precision=largest_value
        )
        return (
            total
            + jnp.einsum("gri,gkip->krp", row_select, broadened_width, precision=largest_value),
            None,
        )

    start = jnp.zeros((2, patch_rows, patch_cols), jnp.float32)
    placed, _ = lax.scan(place_group, start, (pairs, grouped_offsets))
    return (placed[0], placed[1])


def shards(
    exposures, variance, mask_bits, kernel_coeffs, ccd_visit, strip_patch, strip_row, strip_col
):
    ccd_count, height, columns = exposures.shape
    strip_total = strip_patch.shape[0]
    per_ccd = strip_total // ccd_count
    strip_rows = height // per_ccd
    devices = lax.axis_size("patch")
    capacity = 2 * strip_total // devices
    kernel_half_width = KS // 2
    usable = (jnp.bitwise_and(mask_bits, 3) != 3).astype(jnp.float32)
    visit_hot = (ccd_visit == jnp.arange(VISITS)[None, :]).astype(jnp.float32)
    local_count = jnp.sum(jnp.sum(usable, axis=(1, 2))[:, None] * visit_hot, axis=0)
    local_load = jnp.sum(jnp.sum(usable * variance, axis=(1, 2))[:, None] * visit_hot, axis=0)
    visit_count, visit_load = lax.psum((local_count, local_load), "patch")
    visit_weight = (visit_count + 1.0) / (visit_load + 1.0)
    detector_weight = jnp.sum(visit_hot * visit_weight[None, :], axis=1)
    destination = strip_patch[:, 0]
    strip_ids = jnp.arange(strip_total)
    earlier = strip_ids[None, :] < strip_ids[:, None]
    same_target = destination[None, :] == destination[:, None]
    slot_rank = jnp.sum(jnp.logical_and(earlier, same_target).astype(jnp.int32), axis=1)
    slot_index = destination * capacity + slot_rank
    strip_visit = jnp.repeat(ccd_visit[:, 0], per_ccd)
    placement = jnp.stack([strip_row, strip_col, strip_visit], axis=1)

    def pack(values):
        holder = jnp.zeros((devices * capacity,) + values.shape[1:], values.dtype)
        return holder.at[slot_index].set(values).reshape((devices, capacity) + values.shape[1:])

    plane_weight = detector_weight[:, None, None] * usable
    padded = jnp.pad(exposures, ((0, 0), (kernel_half_width, kernel_half_width), (0, 0)))
    weight_strips = plane_weight.reshape(strip_total, strip_rows, columns)

    def match_ccd(ccd_pair):
        return convolve(ccd_pair[0][None], ccd_pair[1][None], height)[0]

    convolved = lax.map(match_ccd, (padded, kernel_coeffs))
    flux_strips = (plane_weight * convolved).reshape(strip_total, strip_rows, columns)
    flux_slots, weight_slots, slot_meta = (
        lax.all_to_all(pack(flux_strips), "patch", split_axis=0, concat_axis=0, tiled=True),
        lax.all_to_all(pack(weight_strips), "patch", split_axis=0, concat_axis=0, tiled=True),
        lax.all_to_all(pack(placement), "patch", split_axis=0, concat_axis=0, tiled=True),
    )
    slot_total = flux_slots.shape[0] * flux_slots.shape[1]
    flux_flat = flux_slots.reshape(slot_total, strip_rows, columns)
    weight_flat = weight_slots.reshape(slot_total, strip_rows, columns)
    meta_flat = slot_meta.reshape(slot_total, 3)
    numerator, weight_map = place_slots(flux_flat, weight_flat, meta_flat, PH, PW)
    coadd_image = numerator / jnp.maximum(weight_map, 1.0)
    return (coadd_image[None], weight_map[None])


def solution(mesh):
    return jax.shard_map(
        shards,
        mesh=mesh,
        in_specs=(
            P(("band", "patch"), None, None),
            P(("band", "patch"), None, None),
            P(("band", "patch"), None, None),
            P(("band", "patch"), None, None),
            P(("band", "patch"), None),
            P(("band", "patch"), None),
            P(("band", "patch")),
            P(("band", "patch")),
        ),
        out_specs=(P(("band", "patch"), None, None), P(("band", "patch"), None, None)),
        check_vma=False,
    )
```

profile of v0, /device:TPU:1, one launch (start us, length us, event | category | flops | bytes accessed | tf_op | source)
XLA Modules:
  0.0 298.1 jit_solution(13118752357412714813)
XLA Ops:
  0.6 0.9 convert_reduce_fusion.1
  2.2 0.7 broadcast_in_dim.57
  3.8 1.3 scatter_custom_fusion.2
  5.1 13.3 %all-to-all-start.2 = ((s32[64,2,3]{2,1,0:T(2,128)}), s32[64,2,3]{2,1,0:T(2,128)}, u32[]{:S(2)}, u32[]{:S(2)}) async-start(s32[64,2,3]{2,1,0:T(2,128)} %bitcast.48), calls=%async_computation.2 | async-start | bytes 131072 | tf_op jit(solution)/shard_map/all_to_all | solution.py:162
  18.5 1.2 convert_reduce_fusion
  19.7 0.7 select_reduce_fusion.3
  20.4 124.1 %all-reduce.1 = (f32[8]{0:T(128)S(1)}, f32[8]{0:T(128)S(1)}) all-reduce(f32[8]{0:T(128)S(1)} %get-tuple-element.213, f32[8]{0:T(128)S(1)} %get-tuple-element.212), channel_id=1, replica_groups=mesh['patch'=64,'band'=4] {'patch'}, use_global_device_ids=true, to_apply=%region_6.0 | all-reduce | flops 16 | bytes 128 | tf_op jit(solution)/shard_map/psum | solution.py:134
  144.6 0.8 select_reduce_fusion.1
  145.4 1.0 pad.4
  146.4 72.8 %while.28 = (s32[]{:T(128)}, f32[2,256,128]{2,1,0:T(8,128)S(1)}, f32[2,276,128]{2,1,0:T(8,128)S(1)}, f32[2,27,6]{1,0,2:T(2,128)S(1)}) while((s32[]{:T(128)}, f32[2,256,128]{2,1,0:T(8,128)S(1)}, f32[2,276,128]{2,1,0:T(8,128)S(1)}, f32[2,27,6]{1,0,2:T(2,128)S(1)}) %tuple.113), condition=%wide.region_15.16_spmd.clone, body=%wide.region_8.15_spmd.sunk.clone | while | flops 2410444800 | bytes 34224728 | solution.py:157
  147.1 0.8 divide_select_fusion.18
  147.9 0.8 fusion.153
  151.6 0.8 divide_select_fusion.20
  152.4 0.8 fusion.155
  153.2 3.2 %fusion.156 = f32[1,3,3,256,128]{3,4,2,1,0:T(8,128)} fusion(f32[1,3,256,276]{2,3,1,0:T(8,128)S(1)} %maximum_bitcast_fusion.24, f32[1,3,256,276]{2,3,1,0:T(8,128)S(1)} %maximum_bitcast_fusion.25, f32[1,3,256,276]{2,3,1,0:T(8,128)S(1)} %maximum_bitcast_fusion.26, f32[2,276,128]{2,1,0:T(8,128)S(1)} %get-tuple-element.387, s32[]{:T(128)} %get-tuple-element.381), kind=kOutput, calls=%fused_computation.29.clone.1.clone | convolution fusion | flops 978020352 | bytes 3903492 | tf_op jit(solution)/shard_map/while/body/eval_jaxpr/gaij,njc->ngaic/dot_general | solution.py:49
  157.7 1.2 stack.132
  159.2 2.4 fusion.159
  161.6 1.5 copy.124
  164.4 2.5 fusion.161
  167.0 2.4 fusion.162
  169.4 1.5 copy.126
  172.1 2.5 fusion.164
  174.7 2.4 fusion.152
  177.1 1.5 copy.122
  180.0 2.5 fusion.158
  183.4 0.8 divide_select_fusion.18
  184.2 0.8 fusion.153
  187.9 0.8 divide_select_fusion.20
  188.7 0.8 fusion.155
  189.5 3.2 %fusion.156 = f32[1,3,3,256,128]{3,4,2,1,0:T(8,128)} fusion(f32[1,3,256,276]{2,3,1,0:T(8,128)S(1)} %maximum_bitcast_fusion.24, f32[1,3,256,276]{2,3,1,0:T(8,128)S(1)} %maximum_bitcast_fusion.25, f32[1,3,256,276]{2,3,1,0:T(8,128)S(1)} %maximum_bitcast_fusion.26, f32[2,276,128]{2,1,0:T(8,128)S(1)} %get-tuple-element.387, s32[]{:T(128)} %get-tuple-element.381), kind=kOutput, calls=%fused_computation.29.clone.1.clone | convolution fusion | flops 978020352 | bytes 3903492 | tf_op jit(solution)/shard_map/while/body/eval_jaxpr/gaij,njc->ngaic/dot_general | solution.py:49
  194.0 1.2 stack.132
  195.5 2.4 fusion.159
  197.9 1.5 copy.124
  200.7 2.5 fusion.161
  203.3 2.4 fusion.162
  205.7 1.5 copy.126
  208.4 2.5 fusion.164
  211.0 2.4 fusion.152
  213.5 1.5 copy.122
  216.3 2.5 fusion.158
  219.3 0.8 broadcast.1248.clone.1
  220.1 6.4 %scatter_fusion = f32[128,8,128]{2,1,0:T(8,128)} fusion(f32[128,8,128]{2,1,0:T(8,128)} %broadcast.1248.clone.1, s32[64]{0:T(128)S(1)} %fusion.78, f32[64,8,128]{2,1,0:T(8,128)S(1)} %bitcast.238), kind=kCustom, calls=%fused_computation | custom fusion | bytes 786688 | tf_op jit(solution)/shard_map/scatter | solution.py:148
  226.6 10.2 %all-to-all-start = ((f32[64,2,8,128]{3,2,1,0:T(8,128)}), f32[64,2,8,128]{3,2,1,0:T(8,128)S(1)}, u32[]{:S(2)}, u32[]{:S(2)}) async-start(f32[64,2,8,128]{3,2,1,0:T(8,128)} %bitcast.41), calls=%async_computation | async-start | bytes 1048576 | tf_op jit(solution)/shard_map/all_to_all | solution.py:160
  236.8 0.8 broadcast.1248.clone
  237.7 6.5 %scatter_fusion.1 = f32[128,8,128]{2,1,0:T(8,128)} fusion(f32[128,8,128]{2,1,0:T(8,128)} %broadcast.1248.clone, s32[64]{0:T(128)S(1)} %fusion.78, f32[64,8,128]{2,1,0:T(8,128)S(1)} %bitcast.237), kind=kCustom, calls=%fused_computation.1 | custom fusion | bytes 786688 | tf_op jit(solution)/shard_map/scatter | solution.py:148
  244.1 10.4 %all-to-all-done = f32[64,2,8,128]{3,2,1,0:T(8,128)S(1)} async-done(((f32[64,2,8,128]{3,2,1,0:T(8,128)}), f32[64,2,8,128]{3,2,1,0:T(8,128)S(1)}, u32[]{:S(2)}, u32[]{:S(2)}) %all-to-all-start) | async-done | bytes 524320 | tf_op jit(solution)/shard_map/all_to_all | solution.py:160
  254.6 5.7 %all-to-all-start.1 = ((f32[64,2,8,128]{3,2,1,0:T(8,128)}), f32[64,2,8,128]{3,2,1,0:T(8,128)S(1)}, u32[]{:S(2)}, u32[]{:S(2)}) async-start(f32[64,2,8,128]{3,2,1,0:T(8,128)} %bitcast.44), calls=%async_computation.1 | async-start | bytes 1048576 | tf_op jit(solution)/shard_map/all_to_all | solution.py:161
  260.3 1.0 copy.79
  261.3 16.8 %all-to-all-done.1 = f32[64,2,8,128]{3,2,1,0:T(8,128)S(1)} async-done(((f32[64,2,8,128]{3,2,1,0:T(8,128)}), f32[64,2,8,128]{3,2,1,0:T(8,128)S(1)}, u32[]{:S(2)}, u32[]{:S(2)}) %all-to-all-start.1) | async-done | bytes 524320 | tf_op jit(solution)/shard_map/all_to_all | solution.py:161
  278.1 19.0 %while.29 = (s32[]{:T(128)}, f32[2,128,512]{1,2,0:T(8,128)S(1)}, f32[8,16,2,8,128]{4,3,2,1,0:T(8,128)S(1)}, s32[8,16,3]{1,2,0:T(4,128)S(1)}) while((s32[]{:T(128)}, f32[2,128,512]{1,2,0:T(8,128)S(1)}, f32[8,16,2,8,128]{4,3,2,1,0:T(8,128)S(1)}, s32[8,16,3]{1,2,0:T(4,128)S(1)}) %tuple.110), condition=%wide.region_20.21_spmd.clone.clone.clone, body=%wide.region_19.20_spmd.clone.clone.sunk.clone | while | flops 403982464 | bytes 2246471 | solution.py:116
  278.2 1.5 fusion.169
  279.7 0.7 fusion.170
  280.6 1.5 fusion.169
  282.1 0.7 fusion.170
  282.9 1.5 fusion.169
  284.5 0.7 fusion.170
  285.3 1.5 fusion.169
  286.9 0.7 fusion.170
  287.7 1.5 fusion.169
  289.2 0.7 fusion.170
  290.1 1.5 fusion.169
  292.4 1.5 fusion.169
  294.8 1.5 fusion.169
  297.3 0.8 slice_divide_fusion
  (120 shorter events, 24.0 us)
Async XLA Ops:
  0.6 145.7 %copy-start = (f32[2,27,6]{1,0,2:T(2,128)S(1)}, f32[2,27,6]{1,0,2:T(2,128)}, u32[]{:S(2)}) copy-start(f32[2,27,6]{1,0,2:T(2,128)} %param.15) | copy-start | bytes 3892
  5.1 221.5 %all-to-all-start.2 = ((s32[64,2,3]{2,1,0:T(2,128)}), s32[64,2,3]{2,1,0:T(2,128)}, u32[]{:S(2)}, u32[]{:S(2)}) async-start(s32[64,2,3]{2,1,0:T(2,128)} %bitcast.48), calls=%async_computation.2 | async-start | bytes 131072 | tf_op jit(solution)/shard_map/all_to_all | solution.py:162
  226.6 28.0 %all-to-all-start = ((f32[64,2,8,128]{3,2,1,0:T(8,128)}), f32[64,2,8,128]{3,2,1,0:T(8,128)S(1)}, u32[]{:S(2)}, u32[]{:S(2)}) async-start(f32[64,2,8,128]{3,2,1,0:T(8,128)} %bitcast.41), calls=%async_computation | async-start | bytes 1048576 | tf_op jit(solution)/shard_map/all_to_all | solution.py:160
  254.6 23.4 %all-to-all-start.1 = ((f32[64,2,8,128]{3,2,1,0:T(8,128)}), f32[64,2,8,128]{3,2,1,0:T(8,128)S(1)}, u32[]{:S(2)}, u32[]{:S(2)}) async-start(f32[64,2,8,128]{3,2,1,0:T(8,128)} %bitcast.44), calls=%async_computation.1 | async-start | bytes 1048576 | tf_op jit(solution)/shard_map/all_to_all | solution.py:161
where the time goes:
time: 299 us; the launch traced here: 298 us
  blocking collectives  124 us (41%)
  matrix products  53.3 us (18%)
  local copies, waits for them, and re-layouts  33 us (11%)
  other arithmetic  29.5 us (10%)
  starting transfers between devices  29.3 us (10%)
  waiting for transfers between devices  27.2 us (9%)
    psum x1, blocking collectives, shards(): visit_count, visit_load = lax.psum((local_count, local_load), 'patch')  124 us
    all_to_all x1, waiting for transfers between devices, shards(): lax.all_to_all(pack(weight_strips), 'patch', split_axis=0, concat_axis=0,...  16.8 us
    dot_general x6, matrix products, convolve(): jnp.einsum('naic,bcd->nabid', smooth[:, gauss_index], column_ops[gauss_in...  15 us
    dot_general x6, matrix products, convolve(): jnp.einsum('nkp,npid->nkid', kernel_split[:, gauss_index], poly_planes, p...  14.6 us
    scatter x3, local copies, waits for them, and re-layouts, pack(): holder.at[slot_index].set(values)  14.2 us
    all_to_all x1, starting transfers between devices, shards(): lax.all_to_all(pack(placement), 'patch', split_axis=0, concat_axis=0, til...  13.3 us
    dot_general x8, matrix products, place_group(): jnp.einsum('vmwn,vny->vmwy', pixel_block_tile, column_selection, precisio...  11.7 us
    all_to_all x1, waiting for transfers between devices, shards(): lax.all_to_all(pack(flux_strips), 'patch', split_axis=0, concat_axis=0, t...  10.4 us
  transfers between devices with their start and end apart: 3, of which 2 were waited for; matrix products, arithmetic and copies ran while one was open for 31% of the time, Pallas kernels for 0%

commit v1 on v0

v1 whole, which is shorter than its diff:
```python
import functools

import jax
import jax.numpy as jnp
import numpy as np
from jax import lax
from jax.experimental import pallas as pl
from jax.experimental.pallas import tpu as pltpu
from jax.sharding import PartitionSpec as P

PH = 128
PW = 512
KS = 21
VISITS = 8
GAUSS_WIDTHS = (0.75, 1.5, 3.0)
MESH = pl.DeviceIdType.MESH
F32 = jnp.float32
BF16 = jnp.bfloat16

CCDS = 2
CH = 256
CW = 128
SR = 8
STRIPS = 64
DEVS = 64
SLOTS = 2
BLOCK = SLOTS * SR
PLANES = 8
GROUP = DEVS // PLANES
CHUNK = GROUP * BLOCK
COL_SHIFT = 192


def taps(offsets):
    half = KS // 2
    support = np.arange(-half, half + 1, dtype=np.float64)
    inside = np.abs(offsets) <= half
    tables = []
    for spread in GAUSS_WIDTHS:
        total = np.sum(np.exp(-support * support / (2.0 * spread * spread)))
        profile = np.where(inside, np.exp(-offsets * offsets / (2.0 * spread * spread)) / total, 0.0)
        scaled = offsets / spread
        tables += [profile, profile * scaled, profile * scaled * scaled]
    return np.stack(tables)


def tap_matrices():
    rows = np.arange(CH, dtype=np.float64)
    row_ops = taps(rows[None, :] - rows[:, None]).astype(np.float32).reshape(9 * CH, CH)
    cols = np.arange(CW, dtype=np.float64)
    col_ops = taps(cols[:, None] - cols[None, :]).astype(np.float32).reshape(9 * CW, CW)
    high = row_ops.astype(BF16)
    low = (row_ops - high.astype(np.float32)).astype(BF16)
    return high, low, col_ops


def split(x):
    high = x.astype(BF16)
    return high, (x - high.astype(F32)).astype(BF16)


def dot(a, b):
    return jnp.dot(a, b, preferred_element_type=F32)


def kernel(
    mask_h, var_h, exp_h, coef, visit_s, patch, row, col, col_s, rhi_h, rlo_h, cop_h,
    num_o, wgt_o,
    mask, var, expo, rhi, rlo, cop, use, tmp, e_hi, e_lo, s_hi, s_lo, m_hi, m_lo, wk,
    hot, wsend, fsend, msend, wrecv, frecv, mrecv, crep, vrep, rt, rhs, num, wgt,
    load_sem, send_sem, wsem, fsem, msem,
):
    me = lax.axis_index("patch")
    band = lax.axis_index("band")
    my_plane = me // GROUP

    loads = [
        pltpu.make_async_copy(src, dst, load_sem.at[k])
        for k, (src, dst) in enumerate(
            [(mask_h, mask), (var_h, var), (exp_h, expo), (rhi_h, rhi), (rlo_h, rlo), (cop_h, cop)]
        )
    ]
    for load in loads:
        load.start()

    barrier = pltpu.get_barrier_semaphore()

    def greet(k, c):
        pl.semaphore_signal(
            barrier, inc=1, device_id=(lax.rem(me + k, DEVS), band), device_id_type=MESH
        )
        return c

    lax.fori_loop(1, DEVS, greet, 0)

    lane = lax.broadcasted_iota(jnp.int32, (STRIPS, STRIPS), 1)
    sub = lax.broadcasted_iota(jnp.int32, (STRIPS, STRIPS), 0)
    prow = patch[...]
    pfull = jnp.broadcast_to(prow, (STRIPS, STRIPS))
    pcol = jnp.sum(jnp.where(lane == sub, pfull, 0), axis=1, keepdims=True)
    rank = jnp.sum(
        jnp.where((pcol == pfull) & (sub < lane), 1, 0), axis=0, keepdims=True
    )
    slot = prow * SLOTS + rank
    slot_id = lax.broadcasted_iota(jnp.int32, (DEVS * SLOTS, STRIPS), 0)
    hot[...] = (slot_id == slot).astype(F32).astype(BF16)

    def roll_strips(values):
        def one(s, c):
            at = pl.ds(pl.multiple_of(s * SR, SR), SR)
            tmp[at, :] = pltpu.roll(values[at, :], lax.bitwise_and(col_s[s], CW - 1), 1)
            return c

        lax.fori_loop(0, STRIPS, one, 0, unroll=8)

    loads[0].wait()
    use[...] = jnp.where(jnp.bitwise_and(mask[...], 3) != 3, 1.0, 0.0)
    roll_strips(use)
    for i in range(SR):
        wsend[pl.ds(i, DEVS * SLOTS, stride=SR), :] = dot(
            hot[...], tmp[pl.ds(i, STRIPS, stride=SR), :].astype(BF16)
        )

    pl.semaphore_wait(barrier, DEVS - 1)

    def block(d):
        return pl.ds(pl.multiple_of(d * BLOCK, BLOCK), BLOCK)

    def send_all(src, dst, ssem, rsem):
        def one(k, c):
            d = lax.rem(me + k, DEVS)
            pltpu.make_async_remote_copy(
                src_ref=src.at[block(d)],
                dst_ref=dst.at[block(me)],
                send_sem=ssem,
                recv_sem=rsem.at[my_plane],
                device_id=(d, band),
                device_id_type=MESH,
            ).start()
            return c

        lax.fori_loop(1, DEVS, one, 0)
        pltpu.make_async_copy(src.at[block(me)], dst.at[block(me)], rsem.at[my_plane]).start()

    send_all(wsend, wrecv, send_sem.at[0], wsem)

    loads[1].wait()
    lane1 = lax.broadcasted_iota(jnp.int32, (1, CW), 1)
    sums = jnp.zeros((1, CW), F32)
    for c in range(CCDS):
        u = use[c * CH : (c + 1) * CH, :]
        count = jnp.sum(u)
        amount = jnp.sum(u * var[c * CH : (c + 1) * CH, :])
        v = visit_s[c, 0]
        sums = sums + jnp.where(lane1 == v + 16, count, 0.0) + jnp.where(lane1 == v + 24, amount, 0.0)
    strip_lane = lax.broadcasted_iota(jnp.int32, (1, STRIPS), 1)
    vrow = jnp.where(strip_lane < STRIPS // CCDS, visit_s[0, 0], visit_s[1, 0])
    q_sub = lax.broadcasted_iota(jnp.int32, (CW, STRIPS), 0)
    hot_id = lax.broadcasted_iota(jnp.int32, (DEVS, STRIPS), 0)
    meta = jnp.broadcast_to(sums, (DEVS, CW))
    for j in range(SLOTS):
        q = jnp.where(q_sub == 8 * j, row[...], 0)
        q = jnp.where(q_sub == 8 * j + 1, col[...] - COL_SHIFT, q)
        q = jnp.where(q_sub == 8 * j + 2, vrow, q)
        hot_j = (hot_id * SLOTS + j == slot).astype(F32).astype(BF16)
        meta = meta + lax.dot_general(
            hot_j, q.astype(F32).astype(BF16), (((1,), (1,)), ((), ())), preferred_element_type=F32
        )
    msend[...] = meta.reshape(DEVS, 1, CW)

    def send_meta(k, c):
        d = lax.rem(me + k, DEVS)
        pltpu.make_async_remote_copy(
            src_ref=msend.at[d],
            dst_ref=mrecv.at[me],
            send_sem=send_sem.at[1],
            recv_sem=msem,
            device_id=(d, band),
            device_id_type=MESH,
        ).start()
        return c

    lax.fori_loop(1, DEVS, send_meta, 0)
    own_meta = pltpu.make_async_copy(msend.at[me], mrecv.at[me], load_sem.at[6])
    own_meta.start()

    loads[2].wait()
    for c in range(CCDS):
        high, low = split(expo[c * CH : (c + 1) * CH, :])
        e_hi[:, c * CW : (c + 1) * CW] = high
        e_lo[:, c * CW : (c + 1) * CW] = low
    loads[3].wait()
    loads[4].wait()

    def row_pass(k, c):
        at = pl.ds(pl.multiple_of(k * CH, CH), CH)
        to = pl.ds(pl.multiple_of(k * CW, CW), CW)
        s = dot(rhi[at, :], e_hi[...]) + dot(rhi[at, :], e_lo[...]) + dot(rlo[at, :], e_hi[...])
        high, low = split(s)
        for n in range(CCDS):
            s_hi[n, :, to] = high[:, n * CW : (n + 1) * CW]
            s_lo[n, :, to] = low[:, n * CW : (n + 1) * CW]
        return c

    lax.fori_loop(0, 9, row_pass, 0)

    x = 2.0 * lax.broadcasted_iota(jnp.int32, (1, CW), 1).astype(F32) / (CW - 1) - 1.0
    for n in range(CCDS):
        k = coef[n]
        wk[n, 0] = k[:, 0:1] + k[:, 1:2] * x + k[:, 3:4] * (x * x)
        wk[n, 1] = k[:, 2:3] + k[:, 4:5] * x
        wk[n, 2] = jnp.broadcast_to(k[:, 5:6], (27, CW))
    loads[5].wait()

    def column_ops(k, c):
        to = pl.ds(pl.multiple_of(k * CW, CW), CW)
        for n in range(CCDS):
            for p in range(3):
                m = jnp.zeros((CW, CW), F32)
                for b in range(3):
                    at = pl.ds(pl.multiple_of((k // 3 * 3 + b) * CW, CW), CW)
                    m = m + cop[at, :] * wk[n, p, pl.ds(3 * k + b, 1), :]
                high, low = split(m)
                m_hi[n, to, p * CW : (p + 1) * CW] = high
                m_lo[n, to, p * CW : (p + 1) * CW] = low
        return c

    lax.fori_loop(0, 9, column_ops, 0)
    y = 2.0 * lax.broadcasted_iota(jnp.int32, (CH, 1), 0).astype(F32) / (CH - 1) - 1.0
    for n in range(CCDS):
        o = dot(s_hi[n], m_hi[n]) + dot(s_hi[n], m_lo[n]) + dot(s_lo[n], m_hi[n])
        conv = o[:, :CW] + y * o[:, CW : 2 * CW] + (y * y) * o[:, 2 * CW :]
        at = pl.ds(n * CH, CH)
        use[at, :] = use[at, :] * conv

    roll_strips(use)
    for i in range(SR):
        high, low = split(tmp[pl.ds(i, STRIPS, stride=SR), :])
        fsend[pl.ds(i, DEVS * SLOTS, stride=SR), :] = dot(hot[...], high) + dot(hot[...], low)
    send_all(fsend, frecv, send_sem.at[2], fsem)

    own_meta.wait()
    all_meta = pltpu.make_async_remote_copy(
        src_ref=msend.at[pl.ds(0, DEVS - 1)],
        dst_ref=mrecv.at[pl.ds(0, DEVS - 1)],
        send_sem=send_sem.at[1],
        recv_sem=msem,
        device_id=(me, band),
        device_id_type=MESH,
    )
    all_meta.wait_recv()
    got = mrecv[...].reshape(DEVS, CW)
    totals = jnp.sum(got, axis=0, keepdims=True)
    weights = (totals + 1.0) / (pltpu.roll(totals, CW - 8, 1) + 1.0)
    lane_d = lax.broadcasted_iota(jnp.int32, (DEVS, CW), 1)
    for j in range(SLOTS):
        at = pl.ds(j * DEVS, DEVS)
        v = got[:, 8 * j + 2 : 8 * j + 3].astype(jnp.int32)
        vw = jnp.sum(
            jnp.where(lane_d == v + 16, jnp.broadcast_to(weights, (DEVS, CW)), 0.0),
            axis=1,
            keepdims=True,
        )
        rhs[at, 0:CW] = jnp.broadcast_to(got[:, 8 * j + 1 : 8 * j + 2], (DEVS, CW))
        rhs[at, CW : 2 * CW] = jnp.broadcast_to(got[:, 8 * j : 8 * j + 1], (DEVS, CW))
        rhs[at, 2 * CW :] = jnp.broadcast_to(vw, (DEVS, CW))
    spread_in = rhs[...].astype(BF16)
    weights_low = split(rhs[:, 2 * CW :])[1]

    k_sub = lax.broadcasted_iota(jnp.int32, (CHUNK, SLOTS * DEVS), 0)
    k_lane = lax.broadcasted_iota(jnp.int32, (CHUNK, SLOTS * DEVS), 1)
    lane_c = lax.broadcasted_iota(jnp.int32, (CHUNK, CW), 1).astype(F32)
    row_in = (lax.broadcasted_iota(jnp.int32, (CHUNK, CW), 0) % SR).astype(F32)

    def spread(p, c):
        at = pl.ds(pl.multiple_of(p * CHUNK, CHUNK), CHUNK)
        here = (k_lane - p * GROUP == k_sub // BLOCK + (k_sub // SR) % SLOTS * DEVS)
        here = here.astype(F32).astype(BF16)
        full = dot(here, spread_in)
        crep[at, :] = lane_c - (full[:, :CW] + COL_SHIFT)
        rt[at, :] = (lane_c == full[:, CW : 2 * CW] + row_in).astype(F32).astype(BF16)
        vrep[at, :] = full[:, 2 * CW :] + dot(here, weights_low)
        return c

    lax.fori_loop(0, PLANES, spread, 0)

    num[...] = jnp.zeros_like(num)
    wgt[...] = jnp.zeros_like(wgt)

    def place_all(src, recv, rsem, total):
        def one(p, c):
            at = pl.ds(pl.multiple_of(p * CHUNK, CHUNK), CHUNK)
            pltpu.make_async_copy(src.at[at], recv.at[at], rsem.at[p]).wait()
            high, low = split(recv[at, :] * vrep[at, :])
            off = crep[at, :]
            op = rt[at, :]
            zero = jnp.zeros_like(high)
            for t in range(PW // CW):
                away = off + float(t * CW)
                inside = (away >= 0.0) & (away < CW)
                cols = pl.ds(t * CW, CW)
                dims = (((0,), (0,)), ((), ()))
                total[:, cols] += lax.dot_general(
                    op, jnp.where(inside, high, zero), dims, preferred_element_type=F32
                ) + lax.dot_general(
                    op, jnp.where(inside, low, zero), dims, preferred_element_type=F32
                )
            return c

        lax.fori_loop(0, PLANES, one, 0)

    place_all(wsend, wrecv, wsem, wgt)
    place_all(fsend, frecv, fsem, num)
    wgt_o[...] = wgt[...]
    num_o[...] = num[...] / jnp.maximum(wgt[...], 1.0)

    all_meta.wait_send()
    for k, buf in ((0, wsend), (2, fsend)):
        rest = pl.ds(0, (DEVS - 1) * BLOCK)
        pltpu.make_async_copy(buf.at[rest], buf.at[rest], send_sem.at[k]).wait()


def shards(
    exposures, variance, mask_bits, kernel_coeffs, ccd_visit, strip_patch, strip_row, strip_col
):
    rhi, rlo, cop = tap_matrices()
    flat = (CCDS * CH, CW)
    anywhere = pl.BlockSpec(memory_space=pl.ANY)
    vmem = pl.BlockSpec(memory_space=pltpu.VMEM)
    smem = pl.BlockSpec(memory_space=pltpu.SMEM)
    slots = DEVS * BLOCK
    coadd, weight = pl.pallas_call(
        kernel,
        out_shape=[jax.ShapeDtypeStruct((PH, PW), F32)] * 2,
        in_specs=[anywhere] * 3 + [vmem, smem, vmem, vmem, vmem, smem] + [anywhere] * 3,
        out_specs=[vmem, vmem],
        scratch_shapes=[
            pltpu.VMEM(flat, jnp.int32),
            pltpu.VMEM(flat, F32),
            pltpu.VMEM(flat, F32),
            pltpu.VMEM(rhi.shape, BF16),
            pltpu.VMEM(rlo.shape, BF16),
            pltpu.VMEM(cop.shape, F32),
            pltpu.VMEM(flat, F32),
            pltpu.VMEM(flat, F32),
            pltpu.VMEM((CH, CCDS * CW), BF16),
            pltpu.VMEM((CH, CCDS * CW), BF16),
            pltpu.VMEM((CCDS, CH, 9 * CW), BF16),
            pltpu.VMEM((CCDS, CH, 9 * CW), BF16),
            pltpu.VMEM((CCDS, 9 * CW, 3 * CW), BF16),
            pltpu.VMEM((CCDS, 9 * CW, 3 * CW), BF16),
            pltpu.VMEM((CCDS, 3, 27, CW), F32),
            pltpu.VMEM((DEVS * SLOTS, STRIPS), BF16),
            pltpu.VMEM((slots, CW), F32),
            pltpu.VMEM((slots, CW), F32),
            pltpu.VMEM((DEVS, 1, CW), F32),
            pltpu.VMEM((slots, CW), F32),
            pltpu.VMEM((slots, CW), F32),
            pltpu.VMEM((DEVS, 1, CW), F32),
            pltpu.VMEM((slots, CW), F32),
            pltpu.VMEM((slots, CW), F32),
            pltpu.VMEM((slots, CW), BF16),
            pltpu.VMEM((SLOTS * DEVS, 3 * CW), F32),
            pltpu.VMEM((PH, PW), F32),
            pltpu.VMEM((PH, PW), F32),
            pltpu.SemaphoreType.DMA((7,)),
            pltpu.SemaphoreType.DMA((3,)),
            pltpu.SemaphoreType.DMA((PLANES,)),
            pltpu.SemaphoreType.DMA((PLANES,)),
            pltpu.SemaphoreType.DMA,
        ],
        compiler_params=pltpu.CompilerParams(
            collective_id=0, has_side_effects=True, vmem_limit_bytes=48 * 1024 * 1024
        ),
        cost_estimate=pl.CostEstimate(
            flops=2_600_000_000, bytes_accessed=6_000_000, transcendentals=0
        ),
    )(
        mask_bits.reshape(flat),
        variance.reshape(flat),
        exposures.reshape(flat),
        kernel_coeffs,
        ccd_visit,
        strip_patch.reshape(1, STRIPS),
        strip_row.reshape(1, STRIPS),
        strip_col.reshape(1, STRIPS),
        strip_col,
        jnp.asarray(rhi),
        jnp.asarray(rlo),
        jnp.asarray(cop),
    )
    return (coadd[None], weight[None])


def solution(mesh):
    return jax.shard_map(
        shards,
        mesh=mesh,
        in_specs=(
            P(("band", "patch"), None, None),
            P(("band", "patch"), None, None),
            P(("band", "patch"), None, None),
            P(("band", "patch"), None, None),
            P(("band", "patch"), None),
            P(("band", "patch"), None),
            P(("band", "patch")),
            P(("band", "patch")),
        ),
        out_specs=(P(("band", "patch"), None, None), P(("band", "patch"), None, None)),
        check_vma=False,
    )
```

time: 299 us -> 52.4 us (0.18)
  blocking collectives: 124 us -> 0 us
  matrix products: 53.3 us -> 0 us
  Pallas kernels: 0 us -> 40 us
  other arithmetic: 29.5 us -> 0 us
  starting transfers between devices: 29.3 us -> 0 us
  waiting for transfers between devices: 27.2 us -> 0 us
  local copies, waits for them, and re-layouts: 33 us -> 11.4 us
    psum x1 -> x0, blocking collectives: 124 us -> none  [shards(): visit_count, visit_load = lax.psum((local_count, local_load), 'patch')]
    dot_general x30 -> x0, matrix products: 53.3 us -> none  [the longest x6 15 us: convolve(): jnp.einsum('naic,bcd->nabid', smooth[:, gauss_index], column_ops[gauss_in...]
    pallas_call x0 -> x1, Pallas kernels: none -> 40 us  [shards(): pl.pallas_call(kernel, out_shape=[jax.ShapeDtypeStruct((PH, PW), F32)] *...]
    all_to_all x3 -> x0, starting transfers between devices: 29.3 us -> none  [the longest x1 13.3 us: shards(): lax.all_to_all(pack(placement), 'patch', split_axis=0, concat_axis=0, til...]
    all_to_all x3 -> x0, waiting for transfers between devices: 27.2 us -> none  [the longest x1 16.8 us: shards(): lax.all_to_all(pack(weight_strips), 'patch', split_axis=0, concat_axis=0,...]
    mul x31 -> x0, other arithmetic: 17.9 us -> none  [the longest x12 8.58 us: tap_values(): jnp.exp(-offsets * offsets / (2.0 * spread * spread)) / gauss_total * inside]
    scatter x3 -> x0, local copies, waits for them, and re-layouts: 14.2 us -> none  [pack(): holder.at[slot_index].set(values)]
    unnamed x3 -> x22, local copies, waits for them, and re-layouts: 0.96 us -> 11.4 us
  transfers between devices with their start and end apart: 3 -> 0, of which waited for: 2 -> 0; matrix products, arithmetic and copies ran while one was open for 31% -> 0% of each run, Pallas kernels for 0% -> 0%
where the time goes in v1:
time: 52.4 us; the launch traced here: 52 us
  Pallas kernels  40 us (76%)
  local copies, waits for them, and re-layouts  11.4 us (22%)
  between operations  0.65 us (1%)
    pallas_call x1, Pallas kernels, shards(): pl.pallas_call(kernel, out_shape=[jax.ShapeDtypeStruct((PH, PW), F32)] *...  40 us
    unnamed x22, local copies, waits for them, and re-layouts  11.4 us

profile of v1, /device:TPU:1, one launch (start us, length us, event | category | flops | bytes accessed | tf_op | source)
XLA Modules:
  0.0 52.0 jit_solution(5212571534419584071)
XLA Ops:
  0.6 0.7 %copy.14.visit_s = s32[2,1]{1,0:T(2,128)S(1)} copy(s32[2,1]{0,1:T(1,128)} %param.15) | data formatting | bytes 16 | tf_op args[4]
  1.4 0.8 %copy.13.coef = f32[2,27,6]{2,1,0:T(8,128)S(1)} copy(f32[2,27,6]{1,0,2:T(2,128)} %param.14) | data formatting | bytes 2592 | tf_op args[3]
  2.2 0.0 copy-start
  2.2 1.0 %copy-done = s32[2,256,128]{2,1,0:T(8,128)S(1)} copy-done((s32[2,256,128]{2,1,0:T(8,128)S(1)}, s32[2,256,128]{2,1,0:T(8,128)}, u32[]{:S(2)}) %copy-start) | copy-done | bytes 262168
  3.1 0.0 copy-start.1
  3.1 0.9 %copy-done.1 = f32[2,256,128]{2,1,0:T(8,128)S(1)} copy-done((f32[2,256,128]{2,1,0:T(8,128)S(1)}, f32[2,256,128]{2,1,0:T(8,128)}, u32[]{:S(2)}) %copy-start.1) | copy-done | bytes 262168
  4.1 0.0 copy-start.2
  4.1 0.9 %copy-done.2 = f32[2,256,128]{2,1,0:T(8,128)S(1)} copy-done((f32[2,256,128]{2,1,0:T(8,128)S(1)}, f32[2,256,128]{2,1,0:T(8,128)}, u32[]{:S(2)}) %copy-start.2) | copy-done | bytes 262168
  5.0 0.0 copy-start.3
  5.0 0.7 %copy-done.3 = s32[64,1]{0,1:T(1,128)S(1)} copy-done((s32[64,1]{0,1:T(1,128)S(1)}, s32[64,1]{0,1:T(1,128)}, u32[]{:S(2)}) %copy-start.3) | copy-done | bytes 280
  5.7 0.0 copy-start.4
  5.7 0.7 %copy-done.4 = s32[64]{0:T(128)S(1)} copy-done((s32[64]{0:T(128)S(1)}, s32[64]{0:T(128)}, u32[]{:S(2)}) %copy-start.4) | copy-done | bytes 280
  6.3 0.0 copy-start.5
  6.3 0.7 %copy-done.5 = s32[64]{0:T(128)S(1)} copy-done((s32[64]{0:T(128)S(1)}, s32[64]{0:T(128)}, u32[]{:S(2)}) %copy-start.5) | copy-done | bytes 280
  7.0 0.0 copy-start.6
  7.0 1.3 %copy-done.6 = bf16[2304,256]{1,0:T(8,128)(2,1)S(1)} copy-done((bf16[2304,256]{1,0:T(8,128)(2,1)S(1)}, bf16[2304,256]{1,0:T(8,128)(2,1)}, u32[]{:S(2)}) %copy-start.6) | copy-done | bytes 1179672
  8.3 0.0 copy-start.7
  8.3 1.3 %copy-done.7 = bf16[2304,256]{1,0:T(8,128)(2,1)S(1)} copy-done((bf16[2304,256]{1,0:T(8,128)(2,1)S(1)}, bf16[2304,256]{1,0:T(8,128)(2,1)}, u32[]{:S(2)}) %copy-start.7) | copy-done | bytes 1179672
  9.5 0.0 copy-start.8
  9.5 1.1 %copy-done.8 = f32[1152,128]{1,0:T(8,128)S(1)} copy-done((f32[1152,128]{1,0:T(8,128)S(1)}, f32[1152,128]{1,0:T(8,128)}, u32[]{:S(2)}) %copy-start.8) | copy-done | bytes 589848
  10.6 40.0 %shard_map.122 = (f32[128,512]{1,0:T(8,128)S(1)}, f32[128,512]{1,0:T(8,128)S(1)}) custom-call(s32[512,128]{1,0:T(8,128)S(1)} %bitcast.10, f32[512,128]{1,0:T(8,128)S(1)} %bitcast.11, f32[512,128]{1,0:T(8,128)S(1)} %bitcast.12, f32[2,27,6]{2,1,0:T(8,128)S(1)} %copy.13.coef, s32[2,1]{1,0:T(2,128)S(1)} %copy.14.visit_s, s32[1,64]{1,0:T(1,128)S(1)} %bitcast.13, ...), custom_call_target="tpu_custom_call" | custom-call | flops 2600000000 | bytes 6000000 | tf_op jit(solution)/shard_map/pallas_call | solution.py:332
  50.6 0.7 %copy.17 = f32[1,128,512]{2,1,0:T(8,128)} copy(f32[1,128,512]{2,1,0:T(8,128)S(1)} %bitcast.9) | data formatting | bytes 524288
  51.3 0.7 %copy.18 = f32[1,128,512]{2,1,0:T(8,128)} copy(f32[1,128,512]{2,1,0:T(8,128)S(1)} %bitcast.8) | data formatting | bytes 524288
Async XLA Ops:
  2.2 1.0 %copy-start = (s32[2,256,128]{2,1,0:T(8,128)S(1)}, s32[2,256,128]{2,1,0:T(8,128)}, u32[]{:S(2)}) copy-start(s32[2,256,128]{2,1,0:T(8,128)} %param.13) | copy-start | bytes 786436
  3.1 0.9 %copy-start.1 = (f32[2,256,128]{2,1,0:T(8,128)S(1)}, f32[2,256,128]{2,1,0:T(8,128)}, u32[]{:S(2)}) copy-start(f32[2,256,128]{2,1,0:T(8,128)} %param.12) | copy-start | bytes 786436
  4.1 0.9 %copy-start.2 = (f32[2,256,128]{2,1,0:T(8,128)S(1)}, f32[2,256,128]{2,1,0:T(8,128)}, u32[]{:S(2)}) copy-start(f32[2,256,128]{2,1,0:T(8,128)} %param.11) | copy-start | bytes 786436
  5.0 0.7 %copy-start.3 = (s32[64,1]{0,1:T(1,128)S(1)}, s32[64,1]{0,1:T(1,128)}, u32[]{:S(2)}) copy-start(s32[64,1]{0,1:T(1,128)} %param.16) | copy-start | bytes 772
  5.7 0.7 %copy-start.4 = (s32[64]{0:T(128)S(1)}, s32[64]{0:T(128)}, u32[]{:S(2)}) copy-start(s32[64]{0:T(128)} %param.17) | copy-start | bytes 772
  6.3 0.7 %copy-start.5 = (s32[64]{0:T(128)S(1)}, s32[64]{0:T(128)}, u32[]{:S(2)}) copy-start(s32[64]{0:T(128)} %col_s.1) | copy-start | bytes 772
  7.0 1.3 %copy-start.6 = (bf16[2304,256]{1,0:T(8,128)(2,1)S(1)}, bf16[2304,256]{1,0:T(8,128)(2,1)}, u32[]{:S(2)}) copy-start(bf16[2304,256]{1,0:T(8,128)(2,1)} %constant.7.clone.rlo_h) | copy-start | bytes 3538948
  8.3 1.3 %copy-start.7 = (bf16[2304,256]{1,0:T(8,128)(2,1)S(1)}, bf16[2304,256]{1,0:T(8,128)(2,1)}, u32[]{:S(2)}) copy-start(bf16[2304,256]{1,0:T(8,128)(2,1)} %constant.6.clone.rhi_h) | copy-start | bytes 3538948
  9.5 1.1 %copy-start.8 = (f32[1152,128]{1,0:T(8,128)S(1)}, f32[1152,128]{1,0:T(8,128)}, u32[]{:S(2)}) copy-start(f32[1152,128]{1,0:T(8,128)} %constant.8.clone.cop_h) | copy-start | bytes 1769476

commit v2 on v1

--- a/solution.py
+++ b/solution.py
@@ -23,6 +23,7 @@
 SR = 8
 STRIPS = 64
 DEVS = 64
+NB = 27
 SLOTS = 2
 BLOCK = SLOTS * SR
 PLANES = 8
@@ -64,10 +65,10 @@
 
 
 def kernel(
-    mask_h, var_h, exp_h, coef, visit_s, patch, row, col, col_s, rhi_h, rlo_h, cop_h,
+    mask_h, var_h, exp_h, coef_h, visit_h, patch_h, row_h, col_h, rhi_h, rlo_h, cop_h,
     num_o, wgt_o,
-    mask, var, expo, rhi, rlo, cop, use, tmp, e_hi, e_lo, s_hi, s_lo, m_hi, m_lo, wk,
-    hot, wsend, fsend, msend, wrecv, frecv, mrecv, crep, vrep, rt, rhs, num, wgt,
+    coef, visit_s, patch, row, col, col_s, mask, var, expo, rhi, rlo, cop, use, flux, tmp, e_hi, e_lo, s_hi, s_lo, m_hi, m_lo, wk,
+    hot, wsend, fsend, msend, wrecv, frecv, mrecv, crep, vrep, rows_of, wide, rhs, num, wgt,
     load_sem, send_sem, wsem, fsem, msem,
 ):
     me = lax.axis_index("patch")
@@ -77,10 +78,23 @@
     loads = [
         pltpu.make_async_copy(src, dst, load_sem.at[k])
         for k, (src, dst) in enumerate(
-            [(mask_h, mask), (var_h, var), (exp_h, expo), (rhi_h, rhi), (rlo_h, rlo), (cop_h, cop)]
+            [
+                (patch_h, patch),
+                (mask_h, mask),
+                (col_h, col_s),
+                (row_h, row),
+                (col_h, col),
+                (visit_h, visit_s),
+                (var_h, var),
+                (exp_h, expo),
+                (coef_h, coef),
+                (cop_h, cop),
+                (rhi_h, rhi),
+                (rlo_h, rlo),
+            ]
         )
     ]
-    for load in loads:
+    for load in loads[:3]:
         load.start()
 
     barrier = pltpu.get_barrier_semaphore()
@@ -92,7 +106,10 @@
         return c
 
     lax.fori_loop(1, DEVS, greet, 0)
-
+    for load in loads[3:]:
+        load.start()
+
+    loads[0].wait()
     lane = lax.broadcasted_iota(jnp.int32, (STRIPS, STRIPS), 1)
     sub = lax.broadcasted_iota(jnp.int32, (STRIPS, STRIPS), 0)
     prow = patch[...]
@@ -108,12 +125,13 @@
     def roll_strips(values):
         def one(s, c):
             at = pl.ds(pl.multiple_of(s * SR, SR), SR)
-            tmp[at, :] = pltpu.roll(values[at, :], lax.bitwise_and(col_s[s], CW - 1), 1)
+            tmp[at, :] = pltpu.roll(values[at, :], lax.bitwise_and(col_s[0, s], CW - 1), 1)
             return c
 
         lax.fori_loop(0, STRIPS, one, 0, unroll=8)
 
-    loads[0].wait()
+    loads[1].wait()
+    loads[2].wait()
     use[...] = jnp.where(jnp.bitwise_and(mask[...], 3) != 3, 1.0, 0.0)
     roll_strips(use)
     for i in range(SR):
@@ -121,14 +139,93 @@
             hot[...], tmp[pl.ds(i, STRIPS, stride=SR), :].astype(BF16)
         )
 
+    def convolve():
+        loads[7].wait()
+        for c in range(CCDS):
+            high, low = split(expo[c * CH : (c + 1) * CH, :])
+            e_hi[:, c * CW : (c + 1) * CW] = high
+            e_lo[:, c * CW : (c + 1) * CW] = low
+        loads[10].wait()
+        loads[11].wait()
+
+        def row_pass(k, c):
+            at = pl.ds(pl.multiple_of(k * CH, CH), CH)
+            to = pl.ds(pl.multiple_of(k * CW, CW), CW)
+            s = dot(rhi[at, :], e_hi[...]) + dot(rhi[at, :], e_lo[...]) + dot(rlo[at, :], e_hi[...])
+            high, low = split(s)
+            for n in range(CCDS):
+                s_hi[n, :, to] = high[:, n * CW : (n + 1) * CW]
+                s_lo[n, :, to] = low[:, n * CW : (n + 1) * CW]
+            return c
+
+        lax.fori_loop(0, 9, row_pass, 0)
+
+        x = 2.0 * lax.broadcasted_iota(jnp.int32, (1, CW), 1).astype(F32) / (CW - 1) - 1.0
+        loads[8].wait()
+        basis = lax.broadcasted_iota(jnp.int32, (NB, NB), 0) == lax.broadcasted_iota(
+            jnp.int32, (NB, NB), 1
+        )
+
+        def term(n, p):
+            return jnp.sum(
+                jnp.where(basis, jnp.broadcast_to(coef[p, n : n + 1, :], (NB, NB)), 0.0),
+                axis=1,
+                keepdims=True,
+            )
+
+        for n in range(CCDS):
+            k = [term(n, p) for p in range(6)]
+            wk[n, 0] = k[0] + k[1] * x + k[3] * (x * x)
+            wk[n, 1] = k[2] + k[4] * x
+            wk[n, 2] = jnp.broadcast_to(k[5], (NB, CW))
+        loads[9].wait()
+
+        def column_ops(k, c):
+            to = pl.ds(pl.multiple_of(k * CW, CW), CW)
+            for n in range(CCDS):
+                for p in range(3):
+                    m = jnp.zeros((CW, CW), F32)
+                    for b in range(3):
+                        at = pl.ds(pl.multiple_of((k // 3 * 3 + b) * CW, CW), CW)
+                        m = m + cop[at, :] * wk[n, p, pl.ds(3 * k + b, 1), :]
+                    high, low = split(m)
+                    m_hi[n, to, p * CW : (p + 1) * CW] = high
+                    m_lo[n, to, p * CW : (p + 1) * CW] = low
+            return c
+
+        lax.fori_loop(0, 9, column_ops, 0)
+        y = 2.0 * lax.broadcasted_iota(jnp.int32, (CH, 1), 0).astype(F32) / (CH - 1) - 1.0
+        for n in range(CCDS):
+            o = dot(s_hi[n], m_hi[n]) + dot(s_hi[n], m_lo[n]) + dot(s_lo[n], m_hi[n])
+            conv = o[:, :CW] + y * o[:, CW : 2 * CW] + (y * y) * o[:, 2 * CW :]
+            at = pl.ds(n * CH, CH)
+            flux[at, :] = use[at, :] * conv
+
+    early = me < DEVS // 2
+
+    @pl.when(early)
+    def _():
+        convolve()
+
     pl.semaphore_wait(barrier, DEVS - 1)
 
     def block(d):
         return pl.ds(pl.multiple_of(d * BLOCK, BLOCK), BLOCK)
 
+    def each(half, act):
+        def one(k, c):
+            d = half * (DEVS // 2) + lax.rem(me + k, DEVS // 2)
+
+            @pl.when(d != me)
+            def _():
+                act(d)
+
+            return c
+
+        lax.fori_loop(0, DEVS // 2, one, 0)
+
     def send_all(src, dst, ssem, rsem):
-        def one(k, c):
-            d = lax.rem(me + k, DEVS)
+        def one(d):
             pltpu.make_async_remote_copy(
                 src_ref=src.at[block(d)],
                 dst_ref=dst.at[block(me)],
@@ -137,24 +234,25 @@
                 device_id=(d, band),
                 device_id_type=MESH,
             ).start()
-            return c
-
-        lax.fori_loop(1, DEVS, one, 0)
+
+        each(0, one)
+        each(1, one)
         pltpu.make_async_copy(src.at[block(me)], dst.at[block(me)], rsem.at[my_plane]).start()
 
     send_all(wsend, wrecv, send_sem.at[0], wsem)
 
-    loads[1].wait()
+    for load in loads[3:7]:
+        load.wait()
     lane1 = lax.broadcasted_iota(jnp.int32, (1, CW), 1)
     sums = jnp.zeros((1, CW), F32)
     for c in range(CCDS):
         u = use[c * CH : (c + 1) * CH, :]
         count = jnp.sum(u)
         amount = jnp.sum(u * var[c * CH : (c + 1) * CH, :])
-        v = visit_s[c, 0]
+        v = visit_s[0, c]
         sums = sums + jnp.where(lane1 == v + 16, count, 0.0) + jnp.where(lane1 == v + 24, amount, 0.0)
     strip_lane = lax.broadcasted_iota(jnp.int32, (1, STRIPS), 1)
-    vrow = jnp.where(strip_lane < STRIPS // CCDS, visit_s[0, 0], visit_s[1, 0])
+    vrow = jnp.where(strip_lane < STRIPS // CCDS, visit_s[0, 0], visit_s[0, 1])
     q_sub = lax.broadcasted_iota(jnp.int32, (CW, STRIPS), 0)
     hot_id = lax.broadcasted_iota(jnp.int32, (DEVS, STRIPS), 0)
     meta = jnp.broadcast_to(sums, (DEVS, CW))
@@ -181,59 +279,14 @@
         return c
 
     lax.fori_loop(1, DEVS, send_meta, 0)
-    own_meta = pltpu.make_async_copy(msend.at[me], mrecv.at[me], load_sem.at[6])
+    own_meta = pltpu.make_async_copy(msend.at[me], mrecv.at[me], load_sem.at[12])
     own_meta.start()
 
-    loads[2].wait()
-    for c in range(CCDS):
-        high, low = split(expo[c * CH : (c + 1) * CH, :])
-        e_hi[:, c * CW : (c + 1) * CW] = high
-        e_lo[:, c * CW : (c + 1) * CW] = low
-    loads[3].wait()
-    loads[4].wait()
-
-    def row_pass(k, c):
-        at = pl.ds(pl.multiple_of(k * CH, CH), CH)
-        to = pl.ds(pl.multiple_of(k * CW, CW), CW)
-        s = dot(rhi[at, :], e_hi[...]) + dot(rhi[at, :], e_lo[...]) + dot(rlo[at, :], e_hi[...])
-        high, low = split(s)
-        for n in range(CCDS):
-            s_hi[n, :, to] = high[:, n * CW : (n + 1) * CW]
-            s_lo[n, :, to] = low[:, n * CW : (n + 1) * CW]
-        return c
-
-    lax.fori_loop(0, 9, row_pass, 0)
-
-    x = 2.0 * lax.broadcasted_iota(jnp.int32, (1, CW), 1).astype(F32) / (CW - 1) - 1.0
-    for n in range(CCDS):
-        k = coef[n]
-        wk[n, 0] = k[:, 0:1] + k[:, 1:2] * x + k[:, 3:4] * (x * x)
-        wk[n, 1] = k[:, 2:3] + k[:, 4:5] * x
-        wk[n, 2] = jnp.broadcast_to(k[:, 5:6], (27, CW))
-    loads[5].wait()
-
-    def column_ops(k, c):
-        to = pl.ds(pl.multiple_of(k * CW, CW), CW)
-        for n in range(CCDS):
-            for p in range(3):
-                m = jnp.zeros((CW, CW), F32)
-                for b in range(3):
-                    at = pl.ds(pl.multiple_of((k // 3 * 3 + b) * CW, CW), CW)
-                    m = m + cop[at, :] * wk[n, p, pl.ds(3 * k + b, 1), :]
-                high, low = split(m)
-                m_hi[n, to, p * CW : (p + 1) * CW] = high
-                m_lo[n, to, p * CW : (p + 1) * CW] = low
-        return c
-
-    lax.fori_loop(0, 9, column_ops, 0)
-    y = 2.0 * lax.broadcasted_iota(jnp.int32, (CH, 1), 0).astype(F32) / (CH - 1) - 1.0
-    for n in range(CCDS):
-        o = dot(s_hi[n], m_hi[n]) + dot(s_hi[n], m_lo[n]) + dot(s_lo[n], m_hi[n])
-        conv = o[:, :CW] + y * o[:, CW : 2 * CW] + (y * y) * o[:, 2 * CW :]
-        at = pl.ds(n * CH, CH)
-        use[at, :] = use[at, :] * conv
-
-    roll_strips(use)
+    @pl.when(jnp.logical_not(early))
+    def _():
+        convolve()
+
+    roll_strips(flux)
     for i in range(SR):
         high, low = split(tmp[pl.ds(i, STRIPS, stride=SR), :])
         fsend[pl.ds(i, DEVS * SLOTS, stride=SR), :] = dot(hot[...], high) + dot(hot[...], low)
@@ -278,7 +331,10 @@
         here = here.astype(F32).astype(BF16)
         full = dot(here, spread_in)
         crep[at, :] = lane_c - (full[:, :CW] + COL_SHIFT)
-        rt[at, :] = (lane_c == full[:, CW : 2 * CW] + row_in).astype(F32).astype(BF16)
+        rt = (lane_c == full[:, CW : 2 * CW] + row_in).astype(F32)
+        turned = jnp.transpose(rt).astype(BF16)
+        rows_of[p, :, 0:CHUNK] = turned
+        rows_of[p, :, CHUNK : 2 * CHUNK] = turned
         vrep[at, :] = full[:, 2 * CW :] + dot(here, weights_low)
         return c
 
@@ -293,18 +349,14 @@
             pltpu.make_async_copy(src.at[at], recv.at[at], rsem.at[p]).wait()
             high, low = split(recv[at, :] * vrep[at, :])
             off = crep[at, :]
-            op = rt[at, :]
             zero = jnp.zeros_like(high)
             for t in range(PW // CW):
                 away = off + float(t * CW)
                 inside = (away >= 0.0) & (away < CW)
                 cols = pl.ds(t * CW, CW)
-                dims = (((0,), (0,)), ((), ()))
-                total[:, cols] += lax.dot_general(
-                    op, jnp.where(inside, high, zero), dims, preferred_element_type=F32
-                ) + lax.dot_general(
-                    op, jnp.where(inside, low, zero), dims, preferred_element_type=F32
-                )
+                wide[0:CHUNK, cols] = jnp.where(inside, high, zero)
+                wide[CHUNK : 2 * CHUNK, cols] = jnp.where(inside, low, zero)
+            total[...] += dot(rows_of[p], wide[...])
             return c
 
         lax.fori_loop(0, PLANES, one, 0)
@@ -312,7 +364,7 @@
     place_all(wsend, wrecv, wsem, wgt)
     place_all(fsend, frecv, fsem, num)
     wgt_o[...] = wgt[...]
-    num_o[...] = num[...] / jnp.maximum(wgt[...], 1.0)
+    num_o[...] = num[...]
 
     all_meta.wait_send()
     for k, buf in ((0, wsend), (2, fsend)):
@@ -325,16 +377,21 @@
 ):
     rhi, rlo, cop = tap_matrices()
     flat = (CCDS * CH, CW)
-    anywhere = pl.BlockSpec(memory_space=pl.ANY)
+    hbm = pl.BlockSpec(memory_space=pltpu.HBM)
     vmem = pl.BlockSpec(memory_space=pltpu.VMEM)
-    smem = pl.BlockSpec(memory_space=pltpu.SMEM)
     slots = DEVS * BLOCK
-    coadd, weight = pl.pallas_call(
+    num, wgt = pl.pallas_call(
         kernel,
         out_shape=[jax.ShapeDtypeStruct((PH, PW), F32)] * 2,
-        in_specs=[anywhere] * 3 + [vmem, smem, vmem, vmem, vmem, smem] + [anywhere] * 3,
+        in_specs=[hbm] * 11,
         out_specs=[vmem, vmem],
         scratch_shapes=[
+            pltpu.VMEM((6, CCDS, NB), F32),
+            pltpu.SMEM((1, CCDS), jnp.int32),
+            pltpu.VMEM((1, STRIPS), jnp.int32),
+            pltpu.VMEM((1, STRIPS), jnp.int32),
+            pltpu.VMEM((1, STRIPS), jnp.int32),
+            pltpu.SMEM((1, STRIPS), jnp.int32),
             pltpu.VMEM(flat, jnp.int32),
             pltpu.VMEM(flat, F32),
             pltpu.VMEM(flat, F32),
@@ -343,13 +400,14 @@
             pltpu.VMEM(cop.shape, F32),
             pltpu.VMEM(flat, F32),
             pltpu.VMEM(flat, F32),
+            pltpu.VMEM(flat, F32),
             pltpu.VMEM((CH, CCDS * CW), BF16),
             pltpu.VMEM((CH, CCDS * CW), BF16),
             pltpu.VMEM((CCDS, CH, 9 * CW), BF16),
             pltpu.VMEM((CCDS, CH, 9 * CW), BF16),
             pltpu.VMEM((CCDS, 9 * CW, 3 * CW), BF16),
             pltpu.VMEM((CCDS, 9 * CW, 3 * CW), BF16),
-            pltpu.VMEM((CCDS, 3, 27, CW), F32),
+            pltpu.VMEM((CCDS, 3, NB, CW), F32),
             pltpu.VMEM((DEVS * SLOTS, STRIPS), BF16),
             pltpu.VMEM((slots, CW), F32),
             pltpu.VMEM((slots, CW), F32),
@@ -359,37 +417,42 @@
             pltpu.VMEM((DEVS, 1, CW), F32),
             pltpu.VMEM((slots, CW), F32),
             pltpu.VMEM((slots, CW), F32),
-            pltpu.VMEM((slots, CW), BF16),
+            pltpu.VMEM((PLANES, PH, 2 * CHUNK), BF16),
+            pltpu.VMEM((2 * CHUNK, PW), BF16),
             pltpu.VMEM((SLOTS * DEVS, 3 * CW), F32),
             pltpu.VMEM((PH, PW), F32),
             pltpu.VMEM((PH, PW), F32),
-            pltpu.SemaphoreType.DMA((7,)),
+            pltpu.SemaphoreType.DMA((13,)),
             pltpu.SemaphoreType.DMA((3,)),
             pltpu.SemaphoreType.DMA((PLANES,)),
             pltpu.SemaphoreType.DMA((PLANES,)),
             pltpu.SemaphoreType.DMA,
         ],
         compiler_params=pltpu.CompilerParams(
-            collective_id=0, has_side_effects=True, vmem_limit_bytes=48 * 1024 * 1024
+            collective_id=0, has_side_effects=True, vmem_limit_bytes=40 * 1024 * 1024
         ),
         cost_estimate=pl.CostEstimate(
             flops=2_600_000_000, bytes_accessed=6_000_000, transcendentals=0
         ),
     )(
-        mask_bits.reshape(flat),
-        variance.reshape(flat),
-        exposures.reshape(flat),
-        kernel_coeffs,
-        ccd_visit,
-        strip_patch.reshape(1, STRIPS),
-        strip_row.reshape(1, STRIPS),
-        strip_col.reshape(1, STRIPS),
-        strip_col,
-        jnp.asarray(rhi),
-        jnp.asarray(rlo),
-        jnp.asarray(cop),
+        *(
+            pltpu.with_memory_space_constraint(operand, pltpu.HBM)
+            for operand in (
+                mask_bits.reshape(flat),
+                variance.reshape(flat),
+                exposures.reshape(flat),
+                kernel_coeffs.transpose(2, 0, 1),
+                ccd_visit.reshape(1, CCDS),
+                strip_patch.reshape(1, STRIPS),
+                strip_row.reshape(1, STRIPS),
+                strip_col.reshape(1, STRIPS),
+                jnp.asarray(rhi),
+                jnp.asarray(rlo),
+                jnp.asarray(cop),
+            )
+        )
     )
-    return (coadd[None], weight[None])
+    return ((num / jnp.maximum(wgt, 1.0))[None], jnp.maximum(wgt, 0.0)[None])
 
 
 def solution(mesh):

time: 52.4 us -> 40.2 us (0.77)
  local copies, waits for them, and re-layouts: 11.4 us -> 0 us
  Pallas kernels: 40 us -> 38.7 us
  other arithmetic: 0 us -> 0.82 us
    unnamed x22 -> x0, local copies, waits for them, and re-layouts: 11.4 us -> none
    pallas_call x1, Pallas kernels: 40 us -> 38.7 us  [shards(): pl.pallas_call(kernel, out_shape=[jax.ShapeDtypeStruct((PH, PW), F32)] *...]
    broadcast_in_dim x0 -> x1, other arithmetic: none -> 0.82 us  [shards(): return ((num / jnp.maximum(wgt, 1.0))[None], jnp.maximum(wgt, 0.0)[None])]
where the time goes in v2:
time: 40.2 us; the launch traced here: 40.1 us
  Pallas kernels  38.7 us (96%)
  other arithmetic  0.82 us (2%)
  between operations  0.64 us (2%)
    pallas_call x1, Pallas kernels, shards(): pl.pallas_call(kernel, out_shape=[jax.ShapeDtypeStruct((PH, PW), F32)] *...  38.7 us
    broadcast_in_dim x1, other arithmetic, shards(): return ((num / jnp.maximum(wgt, 1.0))[None], jnp.maximum(wgt, 0.0)[None])  0.82 us

profile of v2, /device:TPU:1, one launch (start us, length us, event | category | flops | bytes accessed | tf_op | source)
XLA Modules:
  0.0 40.1 jit_solution(13537138128140545686)
XLA Ops:
  0.6 38.7 %shard_map.122 = (f32[128,512]{1,0:T(8,128)S(1)}, f32[128,512]{1,0:T(8,128)S(1)}) custom-call(s32[512,128]{1,0:T(8,128)} %bitcast.12, f32[512,128]{1,0:T(8,128)} %bitcast.13, f32[512,128]{1,0:T(8,128)} %bitcast.14, f32[6,2,27]{2,1,0:T(2,128)} %bitcast.15, s32[1,2]{1,0:T(1,128)} %bitcast.16, s32[1,64]{1,0:T(1,128)} %bitcast.17, s32[1,64]{1,0:T(1,128)} %bitcast.18, ...), custom_call_target="tpu_custom_call" | custom-call | flops 2600000000 | bytes 6000000 | tf_op jit(solution)/shard_map/pallas_call | solution.py:383
  39.3 0.8 %maximum_bitcast_fusion = (f32[1,128,512]{2,1,0:T(8,128)}, f32[1,128,512]{2,1,0:T(8,128)}) fusion(f32[128,512]{1,0:T(8,128)S(1)} %get-tuple-element.5, f32[128,512]{1,0:T(8,128)S(1)} %get-tuple-element.4), kind=kLoop, calls=%fused_computation | loop fusion | flops 196608 | bytes 1048576 | tf_op jit(solution)/shard_map/broadcast_in_dim | solution.py:455

commit v3 on v2

v3 whole, which is shorter than its diff:
```python
import functools

import jax
import jax.numpy as jnp
import numpy as np
from jax import lax
from jax.experimental import pallas as pl
from jax.experimental.pallas import tpu as pltpu
from jax.sharding import PartitionSpec as P

PH = 128
PW = 512
KS = 21
VISITS = 8
GAUSS_WIDTHS = (0.75, 1.5, 3.0)
MESH = pl.DeviceIdType.MESH
F32 = jnp.float32
BF16 = jnp.bfloat16

CCDS = 2
CH = 256
CW = 128
SR = 8
STRIPS = 64
DEVS = 64
NB = 27
SLOTS = 2
BLOCK = SLOTS * SR
PLANES = 8
GROUP = DEVS // PLANES
BANDS = 4
FLUX_ONLY = ("exposures", "row_high", "row_low", "coefficients", "column_taps")
CHUNK = GROUP * BLOCK
COL_SHIFT = 192


def taps(offsets):
    half = KS // 2
    support = np.arange(-half, half + 1, dtype=np.float64)
    inside = np.abs(offsets) <= half
    tables = []
    for spread in GAUSS_WIDTHS:
        total = np.sum(np.exp(-support * support / (2.0 * spread * spread)))
        profile = np.where(inside, np.exp(-offsets * offsets / (2.0 * spread * spread)) / total, 0.0)
        scaled = offsets / spread
        tables += [profile, profile * scaled, profile * scaled * scaled]
    return np.stack(tables)


def tap_matrices():
    rows = np.arange(CH, dtype=np.float64)
    row_ops = taps(rows[None, :] - rows[:, None]).astype(np.float32).reshape(9 * CH, CH)
    cols = np.arange(CW, dtype=np.float64)
    col_ops = taps(cols[:, None] - cols[None, :]).astype(np.float32).reshape(9 * CW, CW)
    high = row_ops.astype(BF16)
    low = (row_ops - high.astype(np.float32)).astype(BF16)
    return high, low, col_ops


def split(x):
    high = x.astype(BF16)
    return high, (x - high.astype(F32)).astype(BF16)


def dot(a, b):
    return jnp.dot(a, b, preferred_element_type=F32)


def kernel(
    flux_mode,
    mask_h, var_h, exp_h, coef_h, visit_h, patch_h, row_h, col_h, rhi_h, rlo_h, cop_h,
    *refs,
):
    if flux_mode:
        num_o, wgt_o, flag_o, *refs = refs
    else:
        wgt_o, *refs = refs
    (
        coef, visit_s, patch, row, col, col_s, mask, var, expo, rhi, rlo, cop,
        use, tmp, e_hi, e_lo, s_hi, s_lo, m_hi, m_lo, wk,
        hot, packed, msend, arrived, mrecv, crep, vrep, rows_of, wide, rhs, placed,
        flag_out, flag_plane, flag_z, flag_band,
        load_sem, send_sem, data_sem, msem, flag_sem,
    ) = refs
    me = lax.axis_index("patch")
    band = lax.axis_index("band")
    my_plane = me // GROUP

    loads = {
        name: pltpu.make_async_copy(src, dst, load_sem.at[k])
        for k, (name, src, dst) in enumerate(
            [
                ("exposures", exp_h, expo),
                ("row_high", rhi_h, rhi),
                ("row_low", rlo_h, rlo),
                ("mask", mask_h, mask),
                ("patch", patch_h, patch),
                ("col_scalar", col_h, col_s),
                ("row", row_h, row),
                ("col", col_h, col),
                ("visit", visit_h, visit_s),
                ("variance", var_h, var),
                ("coefficients", coef_h, coef),
                ("column_taps", cop_h, cop),
            ]
        )
        if flux_mode or name not in FLUX_ONLY
    }
    for load in loads.values():
        load.start()

    barrier = pltpu.get_barrier_semaphore()

    def greet(k, c):
        pl.semaphore_signal(
            barrier, inc=1, device_id=(lax.rem(me + k, DEVS), band), device_id_type=MESH
        )
        return c

    lax.fori_loop(1, DEVS, greet, 0)
    if flux_mode:
        for k in range(1, BANDS):
            pl.semaphore_signal(
                barrier, inc=1, device_id=(me, lax.rem(band + k, BANDS)), device_id_type=MESH
            )
    greeted = DEVS - 1 + (BANDS - 1 if flux_mode else 0)

    if flux_mode:
        loads["exposures"].wait()
        for c in range(CCDS):
            high, low = split(expo[c * CH : (c + 1) * CH, :])
            e_hi[:, c * CW : (c + 1) * CW] = high
            e_lo[:, c * CW : (c + 1) * CW] = low
        loads["row_high"].wait()
        loads["row_low"].wait()

        def row_pass(k, c):
            at = pl.ds(pl.multiple_of(k * CH, CH), CH)
            to = pl.ds(pl.multiple_of(k * CW, CW), CW)
            s = dot(rhi[at, :], e_hi[...]) + dot(rhi[at, :], e_lo[...]) + dot(rlo[at, :], e_hi[...])
            high, low = split(s)
            for n in range(CCDS):
                s_hi[n, :, to] = high[:, n * CW : (n + 1) * CW]
                s_lo[n, :, to] = low[:, n * CW : (n + 1) * CW]
            return c

        lax.fori_loop(0, 9, row_pass, 0)

    loads["patch"].wait()
    lane = lax.broadcasted_iota(jnp.int32, (STRIPS, STRIPS), 1)
    sub = lax.broadcasted_iota(jnp.int32, (STRIPS, STRIPS), 0)
    prow = patch[...]
    pfull = jnp.broadcast_to(prow, (STRIPS, STRIPS))
    pcol = jnp.sum(jnp.where(lane == sub, pfull, 0), axis=1, keepdims=True)
    rank = jnp.sum(
        jnp.where((pcol == pfull) & (sub < lane), 1, 0), axis=0, keepdims=True
    )
    slot = prow * SLOTS + rank
    slot_id = lax.broadcasted_iota(jnp.int32, (DEVS * SLOTS, STRIPS), 0)
    hot[...] = (slot_id == slot).astype(F32).astype(BF16)

    loads["mask"].wait()
    use[...] = jnp.where(jnp.bitwise_and(mask[...], 3) != 3, 1.0, 0.0)
    for name in ("row", "col", "col_scalar", "visit", "variance"):
        loads[name].wait()
    lane1 = lax.broadcasted_iota(jnp.int32, (1, CW), 1)
    sums = jnp.zeros((1, CW), F32)
    usable_count = 0.0
    for c in range(CCDS):
        u = use[c * CH : (c + 1) * CH, :]
        count = jnp.sum(u)
        amount = jnp.sum(u * var[c * CH : (c + 1) * CH, :])
        usable_count = usable_count + count
        v = visit_s[0, c]
        sums = sums + jnp.where(lane1 == v + 16, count, 0.0) + jnp.where(lane1 == v + 24, amount, 0.0)
    strip_lane = lax.broadcasted_iota(jnp.int32, (1, STRIPS), 1)
    vrow = jnp.where(strip_lane < STRIPS // CCDS, visit_s[0, 0], visit_s[0, 1])
    q_sub = lax.broadcasted_iota(jnp.int32, (CW, STRIPS), 0)
    hot_id = lax.broadcasted_iota(jnp.int32, (DEVS, STRIPS), 0)
    meta = jnp.broadcast_to(sums, (DEVS, CW))
    for j in range(SLOTS):
        q = jnp.where(q_sub == 8 * j, row[...], 0)
        q = jnp.where(q_sub == 8 * j + 1, col[...] - COL_SHIFT, q)
        q = jnp.where(q_sub == 8 * j + 2, vrow, q)
        hot_j = (hot_id * SLOTS + j == slot).astype(F32).astype(BF16)
        meta = meta + lax.dot_general(
            hot_j, q.astype(F32).astype(BF16), (((1,), (1,)), ((), ())), preferred_element_type=F32
        )
    msend[...] = meta.reshape(DEVS, 1, CW)

    pl.semaphore_wait(barrier, greeted)

    def send_meta(k):
        d = lax.rem(me + k, DEVS)
        pltpu.make_async_remote_copy(
            src_ref=msend.at[d],
            dst_ref=mrecv.at[me],
            send_sem=send_sem.at[1],
            recv_sem=msem,
            device_id=(d, band),
            device_id_type=MESH,
        ).start()

    own_meta = pltpu.make_async_copy(msend.at[me], mrecv.at[me], load_sem.at[12])
    own_meta.start()

    if flux_mode:
        x = 2.0 * lax.broadcasted_iota(jnp.int32, (1, CW), 1).astype(F32) / (CW - 1) - 1.0
        loads["coefficients"].wait()
        basis = lax.broadcasted_iota(jnp.int32, (NB, NB), 0) == lax.broadcasted_iota(
            jnp.int32, (NB, NB), 1
        )

        def term(n, p):
            return jnp.sum(
                jnp.where(basis, jnp.broadcast_to(coef[p, n : n + 1, :], (NB, NB)), 0.0),
                axis=1,
                keepdims=True,
            )

        for n in range(CCDS):
            k = [term(n, p) for p in range(6)]
            wk[n, 0] = k[0] + k[1] * x + k[3] * (x * x)
            wk[n, 1] = k[2] + k[4] * x
            wk[n, 2] = jnp.broadcast_to(k[5], (NB, CW))
        loads["column_taps"].wait()

        def column_ops(k, c):
            for q in range(7):
                send_meta(7 * k + q + 1)
            to = pl.ds(pl.multiple_of(k * CW, CW), CW)
            for n in range(CCDS):
                for p in range(3):
                    m = jnp.zeros((CW, CW), F32)
                    for b in range(3):
                        at = pl.ds(pl.multiple_of((k // 3 * 3 + b) * CW, CW), CW)
                        m = m + cop[at, :] * wk[n, p, pl.ds(3 * k + b, 1), :]
                    high, low = split(m)
                    m_hi[n, to, p * CW : (p + 1) * CW] = high
                    m_lo[n, to, p * CW : (p + 1) * CW] = low
            return c

        lax.fori_loop(0, 9, column_ops, 0)
        y = 2.0 * lax.broadcasted_iota(jnp.int32, (CH, 1), 0).astype(F32) / (CH - 1) - 1.0
        for n in range(CCDS):
            o = dot(s_hi[n], m_hi[n]) + dot(s_hi[n], m_lo[n]) + dot(s_lo[n], m_hi[n])
            conv = o[:, :CW] + y * o[:, CW : 2 * CW] + (y * y) * o[:, 2 * CW :]
            at = pl.ds(n * CH, CH)
            use[at, :] = use[at, :] * conv
    else:

        def meta_step(k, c):
            send_meta(k)
            return c

        lax.fori_loop(1, DEVS, meta_step, 0)

    def roll_strip(s, c):
        at = pl.ds(pl.multiple_of(s * SR, SR), SR)
        tmp[at, :] = pltpu.roll(use[at, :], lax.bitwise_and(col_s[0, s], CW - 1), 1)
        return c

    lax.fori_loop(0, STRIPS, roll_strip, 0, unroll=8)
    for i in range(SR):
        high, low = split(tmp[pl.ds(i, STRIPS, stride=SR), :])
        packed[pl.ds(i, DEVS * SLOTS, stride=SR), :] = dot(hot[...], high) + dot(hot[...], low)

    def block(d):
        return pl.ds(pl.multiple_of(d * BLOCK, BLOCK), BLOCK)

    def send_half(half):
        def one(k, c):
            d = half * (DEVS // 2) + lax.rem(me + k, DEVS // 2)

            @pl.when(d != me)
            def _():
                pltpu.make_async_remote_copy(
                    src_ref=packed.at[block(d)],
                    dst_ref=arrived.at[block(me)],
                    send_sem=send_sem.at[0],
                    recv_sem=data_sem.at[my_plane],
                    device_id=(d, band),
                    device_id_type=MESH,
                ).start()

            return c

        lax.fori_loop(0, DEVS // 2, one, 0)

    send_half(0)
    send_half(1)
    pltpu.make_async_copy(
        packed.at[block(me)], arrived.at[block(me)], data_sem.at[my_plane]
    ).start()

    def flag_round(r, value, land, mine, peers):
        flag_out[r] = value
        land[mine] = value
        for device_id in peers:
            pltpu.make_async_remote_copy(
                src_ref=flag_out.at[r],
                dst_ref=land.at[mine],
                send_sem=flag_sem.at[0, r],
                recv_sem=flag_sem.at[1, r],
                device_id=device_id,
                device_id_type=MESH,
            ).start()

    def flag_end(r, land):
        n = land.shape[0] - 1
        for k in range(2):
            rest = land.at[pl.ds(0, n)]
            pltpu.make_async_copy(rest, rest, flag_sem.at[k, r]).wait()
        return jnp.max(land[...].reshape(n + 1, CW), axis=0, keepdims=True)

    mine = lax.rem(me, GROUP)
    if flux_mode:
        nonzero = jnp.sum(jnp.where(packed[...] != 0.0, 1.0, 0.0))
        flag = jnp.zeros((1, CW), F32) + (usable_count - nonzero)
        flag_round(
            0, flag, flag_plane, mine,
            [(my_plane * GROUP + lax.rem(mine + k, GROUP), band) for k in range(1, GROUP)],
        )

    own_meta.wait()
    all_meta = pltpu.make_async_remote_copy(
        src_ref=msend.at[pl.ds(0, DEVS - 1)],
        dst_ref=mrecv.at[pl.ds(0, DEVS - 1)],
        send_sem=send_sem.at[1],
        recv_sem=msem,
        device_id=(me, band),
        device_id_type=MESH,
    )
    all_meta.wait_recv()
    if flux_mode:
        flag_round(
            1, flag_end(0, flag_plane), flag_z, my_plane,
            [(lax.rem(me + k * GROUP, DEVS), band) for k in range(1, PLANES)],
        )
    got = mrecv[...].reshape(DEVS, CW)
    totals = jnp.sum(got, axis=0, keepdims=True)
    weights = (totals + 1.0) / (pltpu.roll(totals, CW - 8, 1) + 1.0)
    lane_d = lax.broadcasted_iota(jnp.int32, (DEVS, CW), 1)
    for j in range(SLOTS):
        at = pl.ds(j * DEVS, DEVS)
        v = got[:, 8 * j + 2 : 8 * j + 3].astype(jnp.int32)
        vw = jnp.sum(
            jnp.where(lane_d == v + 16, jnp.broadcast_to(weights, (DEVS, CW)), 0.0),
            axis=1,
            keepdims=True,
        )
        rhs[at, 0:CW] = jnp.broadcast_to(got[:, 8 * j + 1 : 8 * j + 2], (DEVS, CW))
        rhs[at, CW : 2 * CW] = jnp.broadcast_to(got[:, 8 * j : 8 * j + 1], (DEVS, CW))
        rhs[at, 2 * CW :] = jnp.broadcast_to(vw, (DEVS, CW))
    spread_in = rhs[...].astype(BF16)
    weights_low = split(rhs[:, 2 * CW :])[1]

    k_sub = lax.broadcasted_iota(jnp.int32, (CHUNK, SLOTS * DEVS), 0)
    k_lane = lax.broadcasted_iota(jnp.int32, (CHUNK, SLOTS * DEVS), 1)
    lane_c = lax.broadcasted_iota(jnp.int32, (CHUNK, CW), 1).astype(F32)
    row_in = (lax.broadcasted_iota(jnp.int32, (CHUNK, CW), 0) % SR).astype(F32)

    def spread(p, c):
        at = pl.ds(pl.multiple_of(p * CHUNK, CHUNK), CHUNK)
        here = (k_lane - p * GROUP == k_sub // BLOCK + (k_sub // SR) % SLOTS * DEVS)
        here = here.astype(F32).astype(BF16)
        full = dot(here, spread_in)
        crep[at, :] = lane_c - (full[:, :CW] + COL_SHIFT)
        rt = (lane_c == full[:, CW : 2 * CW] + row_in).astype(F32)
        turned = jnp.transpose(rt).astype(BF16)
        rows_of[p, :, 0:CHUNK] = turned
        rows_of[p, :, CHUNK : 2 * CHUNK] = turned
        vrep[at, :] = full[:, 2 * CW :] + dot(here, weights_low)
        return c

    lax.fori_loop(0, PLANES, spread, 0)
    if flux_mode:
        flag_round(
            2, flag_end(1, flag_z), flag_band, band,
            [(me, lax.rem(band + k, BANDS)) for k in range(1, BANDS)],
        )

    placed[...] = jnp.zeros_like(placed)

    def place(p, c):
        at = pl.ds(pl.multiple_of(p * CHUNK, CHUNK), CHUNK)
        pltpu.make_async_copy(packed.at[at], arrived.at[at], data_sem.at[p]).wait()
        value = arrived[at, :]
        weight = vrep[at, :]
        maps = [value * weight]
        if flux_mode:
            maps.append(jnp.where(value != 0.0, weight, 0.0))
        off = crep[at, :]
        for n, (high, low) in enumerate(split(m) for m in maps):
            zero = jnp.zeros_like(high)
            for t in range(PW // CW):
                away = off + float(t * CW)
                inside = (away >= 0.0) & (away < CW)
                cols = pl.ds(n * PW + t * CW, CW)
                wide[0:CHUNK, cols] = jnp.where(inside, high, zero)
                wide[CHUNK : 2 * CHUNK, cols] = jnp.where(inside, low, zero)
        placed[...] += dot(rows_of[p], wide[...])
        return c

    lax.fori_loop(0, PLANES, place, 0)
    if flux_mode:
        num_o[...] = placed[:, :PW]
        wgt_o[...] = placed[:, PW:]
        flag_o[...] = flag_end(2, flag_band)
    else:
        wgt_o[...] = placed[...]

    all_meta.wait_send()
    rest = packed.at[pl.ds(0, (DEVS - 1) * BLOCK)]
    pltpu.make_async_copy(rest, rest, send_sem.at[0]).wait()


def exchange(flux_mode, operands):
    slots = DEVS * BLOCK
    flat = (CCDS * CH, CW)
    hbm = pl.BlockSpec(memory_space=pltpu.HBM)
    vmem = pl.BlockSpec(memory_space=pltpu.VMEM)
    image = jax.ShapeDtypeStruct((PH, PW), F32)
    outs = [image, image, jax.ShapeDtypeStruct((1, CW), F32)] if flux_mode else [image]
    maps = 2 if flux_mode else 1
    return pl.pallas_call(
        functools.partial(kernel, flux_mode),
        out_shape=outs,
        in_specs=[hbm] * 11,
        out_specs=[vmem] * len(outs),
        scratch_shapes=[
            pltpu.VMEM((6, CCDS, NB), F32),
            pltpu.SMEM((1, CCDS), jnp.int32),
            pltpu.VMEM((1, STRIPS), jnp.int32),
            pltpu.VMEM((1, STRIPS), jnp.int32),
            pltpu.VMEM((1, STRIPS), jnp.int32),
            pltpu.SMEM((1, STRIPS), jnp.int32),
            pltpu.VMEM(flat, jnp.int32),
            pltpu.VMEM(flat, F32),
            pltpu.VMEM(flat, F32),
            pltpu.VMEM((9 * CH, CH), BF16),
            pltpu.VMEM((9 * CH, CH), BF16),
            pltpu.VMEM((9 * CW, CW), F32),
            pltpu.VMEM(flat, F32),
            pltpu.VMEM(flat, F32),
            pltpu.VMEM((CH, CCDS * CW), BF16),
            pltpu.VMEM((CH, CCDS * CW), BF16),
            pltpu.VMEM((CCDS, CH, 9 * CW), BF16),
            pltpu.VMEM((CCDS, CH, 9 * CW), BF16),
            pltpu.VMEM((CCDS, 9 * CW, 3 * CW), BF16),
            pltpu.VMEM((CCDS, 9 * CW, 3 * CW), BF16),
            pltpu.VMEM((CCDS, 3, NB, CW), F32),
            pltpu.VMEM((DEVS * SLOTS, STRIPS), BF16),
            pltpu.VMEM((slots, CW), F32),
            pltpu.VMEM((DEVS, 1, CW), F32),
            pltpu.VMEM((slots, CW), F32),
            pltpu.VMEM((DEVS, 1, CW), F32),
            pltpu.VMEM((slots, CW), F32),
            pltpu.VMEM((slots, CW), F32),
            pltpu.VMEM((PLANES, PH, 2 * CHUNK), BF16),
            pltpu.VMEM((2 * CHUNK, maps * PW), BF16),
            pltpu.VMEM((SLOTS * DEVS, 3 * CW), F32),
            pltpu.VMEM((PH, maps * PW), F32),
            pltpu.VMEM((3, 1, CW), F32),
            pltpu.VMEM((GROUP, 1, CW), F32),
            pltpu.VMEM((PLANES, 1, CW), F32),
            pltpu.VMEM((BANDS, 1, CW), F32),
            pltpu.SemaphoreType.DMA((13,)),
            pltpu.SemaphoreType.DMA((2,)),
            pltpu.SemaphoreType.DMA((PLANES,)),
            pltpu.SemaphoreType.DMA,
            pltpu.SemaphoreType.DMA((2, 3)),
        ],
        compiler_params=pltpu.CompilerParams(
            collective_id=0 if flux_mode else 1,
            has_side_effects=True,
            vmem_limit_bytes=40 * 1024 * 1024,
        ),
        cost_estimate=pl.CostEstimate(
            flops=2_600_000_000, bytes_accessed=6_000_000, transcendentals=0
        ),
    )(*(pltpu.with_memory_space_constraint(operand, pltpu.HBM) for operand in operands))


def shards(
    exposures, variance, mask_bits, kernel_coeffs, ccd_visit, strip_patch, strip_row, strip_col
):
    rhi, rlo, cop = tap_matrices()
    flat = (CCDS * CH, CW)
    operands = (
        mask_bits.reshape(flat),
        variance.reshape(flat),
        exposures.reshape(flat),
        kernel_coeffs.transpose(2, 0, 1),
        ccd_visit.reshape(1, CCDS),
        strip_patch.reshape(1, STRIPS),
        strip_row.reshape(1, STRIPS),
        strip_col.reshape(1, STRIPS),
        jnp.asarray(rhi),
        jnp.asarray(rlo),
        jnp.asarray(cop),
    )
    num, wgt, flag = exchange(True, operands)

    def finish(num, wgt):
        return (num / jnp.maximum(wgt, 1.0))[None], jnp.maximum(wgt, 0.0)[None]

    return lax.cond(
        flag[0, 0] > 0.0,
        lambda: finish(num, exchange(False, operands)[0]),
        lambda: finish(num, wgt),
    )


def solution(mesh):
    return jax.shard_map(
        shards,
        mesh=mesh,
        in_specs=(
            P(("band", "patch"), None, None),
            P(("band", "patch"), None, None),
            P(("band", "patch"), None, None),
            P(("band", "patch"), None, None),
            P(("band", "patch"), None),
            P(("band", "patch"), None),
            P(("band", "patch")),
            P(("band", "patch")),
        ),
        out_specs=(P(("band", "patch"), None, None), P(("band", "patch"), None, None)),
        check_vma=False,
    )
```

time: 40.2 us -> 35.9 us (0.89)
  Pallas kernels: 38.7 us -> 34.3 us
    pallas_call x1, Pallas kernels: 38.7 us -> 34.3 us  [exchange(): pl.pallas_call(functools.partial(kernel, flux_mode), out_shape=outs, in_s...]
where the time goes in v3:
time: 35.9 us; the launch traced here: 35.8 us
  Pallas kernels  34.3 us (96%)
  other arithmetic  0.82 us (2%)
  between operations  0.68 us (2%)
    pallas_call x1, Pallas kernels, exchange(): pl.pallas_call(functools.partial(kernel, flux_mode), out_shape=outs, in_s...  34.3 us
    broadcast_in_dim x1, other arithmetic, finish(): return ((num / jnp.maximum(wgt, 1.0))[None], jnp.maximum(wgt, 0.0)[None])  0.82 us

profile of v3, /device:TPU:1, one launch (start us, length us, event | category | flops | bytes accessed | tf_op | source)
XLA Modules:
  0.0 35.8 jit_solution(9481583243957648322)
XLA Ops:
  0.6 34.3 %shard_map.122 = (f32[128,512]{1,0:T(8,128)S(1)}, f32[128,512]{1,0:T(8,128)S(1)}, f32[1,128]{1,0:T(1,128)S(1)}) custom-call(s32[512,128]{1,0:T(8,128)} %bitcast.15, f32[512,128]{1,0:T(8,128)} %bitcast.17, f32[512,128]{1,0:T(8,128)} %bitcast.19, f32[6,2,27]{2,1,0:T(2,128)} %bitcast.21, s32[1,2]{1,0:T(1,128)} %bitcast.23, s32[1,64]{1,0:T(1,128)} %bitcast.25, ...), custom_call_target="tpu_custom_call" | custom-call | flops 2600000000 | bytes 6000000 | tf_op jit(solution)/shard_map/pallas_call | solution.py:426
  35.0 0.8 %maximum_bitcast_fusion = (f32[1,128,512]{2,1,0:T(8,128)}, f32[1,128,512]{2,1,0:T(8,128)}) fusion(f32[128,512]{1,0:T(8,128)S(1)} %get-tuple-element.51, f32[128,512]{1,0:T(8,128)S(1)} %get-tuple-element.50), kind=kLoop, calls=%fused_computation.1 | loop fusion | flops 196608 | bytes 1048576 | tf_op jit(solution)/shard_map/cond/branch_0_fun/broadcast_in_dim | solution.py:506
  (1 shorter events, 0.0 us)

commit v4 on v3

--- a/solution.py
+++ b/solution.py
@@ -78,7 +78,7 @@
     (
         coef, visit_s, patch, row, col, col_s, mask, var, expo, rhi, rlo, cop,
         use, tmp, e_hi, e_lo, s_hi, s_lo, m_hi, m_lo, wk,
-        hot, packed, msend, arrived, mrecv, crep, vrep, rows_of, wide, rhs, placed,
+        hot, packed, msend, mrelay, arrived, mrecv, crep, vrep, rows_of, wide, rhs, placed,
         flag_out, flag_plane, flag_z, flag_band,
         load_sem, send_sem, data_sem, msem, flag_sem,
     ) = refs
@@ -90,18 +90,18 @@
         name: pltpu.make_async_copy(src, dst, load_sem.at[k])
         for k, (name, src, dst) in enumerate(
             [
+                ("coefficients", coef_h, coef),
+                ("column_taps", cop_h, cop),
+                ("patch", patch_h, patch),
+                ("mask", mask_h, mask),
+                ("row", row_h, row),
+                ("col", col_h, col),
+                ("visit", visit_h, visit_s),
+                ("col_scalar", col_h, col_s),
+                ("variance", var_h, var),
                 ("exposures", exp_h, expo),
                 ("row_high", rhi_h, rhi),
                 ("row_low", rlo_h, rlo),
-                ("mask", mask_h, mask),
-                ("patch", patch_h, patch),
-                ("col_scalar", col_h, col_s),
-                ("row", row_h, row),
-                ("col", col_h, col),
-                ("visit", visit_h, visit_s),
-                ("variance", var_h, var),
-                ("coefficients", coef_h, coef),
-                ("column_taps", cop_h, cop),
             ]
         )
         if flux_mode or name not in FLUX_ONLY
@@ -126,25 +126,41 @@
     greeted = DEVS - 1 + (BANDS - 1 if flux_mode else 0)
 
     if flux_mode:
-        loads["exposures"].wait()
-        for c in range(CCDS):
-            high, low = split(expo[c * CH : (c + 1) * CH, :])
-            e_hi[:, c * CW : (c + 1) * CW] = high
-            e_lo[:, c * CW : (c + 1) * CW] = low
-        loads["row_high"].wait()
-        loads["row_low"].wait()
-
-        def row_pass(k, c):
-            at = pl.ds(pl.multiple_of(k * CH, CH), CH)
-            to = pl.ds(pl.multiple_of(k * CW, CW), CW)
-            s = dot(rhi[at, :], e_hi[...]) + dot(rhi[at, :], e_lo[...]) + dot(rlo[at, :], e_hi[...])
-            high, low = split(s)
+        x = 2.0 * lax.broadcasted_iota(jnp.int32, (1, CW), 1).astype(F32) / (CW - 1) - 1.0
+        loads["coefficients"].wait()
+        basis = lax.broadcasted_iota(jnp.int32, (NB, NB), 0) == lax.broadcasted_iota(
+            jnp.int32, (NB, NB), 1
+        )
+
+        def term(n, p):
+            return jnp.sum(
+                jnp.where(basis, jnp.broadcast_to(coef[p, n : n + 1, :], (NB, NB)), 0.0),
+                axis=1,
+                keepdims=True,
+            )
+
+        for n in range(CCDS):
+            k = [term(n, p) for p in range(6)]
+            wk[n, 0] = k[0] + k[1] * x + k[3] * (x * x)
+            wk[n, 1] = k[2] + k[4] * x
+            wk[n, 2] = jnp.broadcast_to(k[5], (NB, CW))
+        loads["column_taps"].wait()
+
+        def column_ops(k, c):
+            to = pl.ds(k * CW, CW)
             for n in range(CCDS):
-                s_hi[n, :, to] = high[:, n * CW : (n + 1) * CW]
-                s_lo[n, :, to] = low[:, n * CW : (n + 1) * CW]
+                for p in range(3):
+                    m = jnp.zeros((CW, CW), F32)
+                    for b in range(3):
+                        at = pl.ds((k // 3 * 3 + b) * CW, CW)
+                        m = m + cop[at, :] * wk[n, p, pl.ds(3 * k + b, 1), :]
+                    high, low = split(m)
+                    m_hi[n, to, p * CW : (p + 1) * CW] = high
+                    m_lo[n, to, p * CW : (p + 1) * CW] = low
             return c
 
-        lax.fori_loop(0, 9, row_pass, 0)
+        for k in range(9):
+            column_ops(k, 0)
 
     loads["patch"].wait()
     lane = lax.broadcasted_iota(jnp.int32, (STRIPS, STRIPS), 1)
@@ -186,81 +202,78 @@
         meta = meta + lax.dot_general(
             hot_j, q.astype(F32).astype(BF16), (((1,), (1,)), ((), ())), preferred_element_type=F32
         )
-    msend[...] = meta.reshape(DEVS, 1, CW)
+    msend[...] = meta.reshape(PLANES, GROUP, 1, CW)
+
+    if flux_mode:
+        loads["exposures"].wait()
+        for c in range(CCDS):
+            high, low = split(expo[c * CH : (c + 1) * CH, :])
+            e_hi[:, c * CW : (c + 1) * CW] = high
+            e_lo[:, c * CW : (c + 1) * CW] = low
+        loads["row_high"].wait()
+        loads["row_low"].wait()
+
+        def row_pass(k, c):
+            at = pl.ds(k * CH, CH)
+            to = pl.ds(k * CW, CW)
+            s = dot(rhi[at, :], e_hi[...]) + dot(rhi[at, :], e_lo[...]) + dot(rlo[at, :], e_hi[...])
+            high, low = split(s)
+            for n in range(CCDS):
+                s_hi[n, :, to] = high[:, n * CW : (n + 1) * CW]
+                s_lo[n, :, to] = low[:, n * CW : (n + 1) * CW]
+            return c
+
+        for k in range(9):
+            row_pass(k, 0)
 
     pl.semaphore_wait(barrier, greeted)
 
-    def send_meta(k):
-        d = lax.rem(me + k, DEVS)
+    mine = lax.rem(me, GROUP)
+    for k in range(1, PLANES):
+        plane = lax.rem(my_plane + k, PLANES)
         pltpu.make_async_remote_copy(
-            src_ref=msend.at[d],
-            dst_ref=mrecv.at[me],
+            src_ref=msend.at[plane],
+            dst_ref=mrelay.at[my_plane],
             send_sem=send_sem.at[1],
-            recv_sem=msem,
-            device_id=(d, band),
+            recv_sem=msem.at[0],
+            device_id=(plane * GROUP + mine, band),
             device_id_type=MESH,
         ).start()
-
-    own_meta = pltpu.make_async_copy(msend.at[me], mrecv.at[me], load_sem.at[12])
-    own_meta.start()
-
-    if flux_mode:
-        x = 2.0 * lax.broadcasted_iota(jnp.int32, (1, CW), 1).astype(F32) / (CW - 1) - 1.0
-        loads["coefficients"].wait()
-        basis = lax.broadcasted_iota(jnp.int32, (NB, NB), 0) == lax.broadcasted_iota(
-            jnp.int32, (NB, NB), 1
-        )
-
-        def term(n, p):
-            return jnp.sum(
-                jnp.where(basis, jnp.broadcast_to(coef[p, n : n + 1, :], (NB, NB)), 0.0),
-                axis=1,
-                keepdims=True,
-            )
-
-        for n in range(CCDS):
-            k = [term(n, p) for p in range(6)]
-            wk[n, 0] = k[0] + k[1] * x + k[3] * (x * x)
-            wk[n, 1] = k[2] + k[4] * x
-            wk[n, 2] = jnp.broadcast_to(k[5], (NB, CW))
-        loads["column_taps"].wait()
-
-        def column_ops(k, c):
-            for q in range(7):
-                send_meta(7 * k + q + 1)
-            to = pl.ds(pl.multiple_of(k * CW, CW), CW)
-            for n in range(CCDS):
-                for p in range(3):
-                    m = jnp.zeros((CW, CW), F32)
-                    for b in range(3):
-                        at = pl.ds(pl.multiple_of((k // 3 * 3 + b) * CW, CW), CW)
-                        m = m + cop[at, :] * wk[n, p, pl.ds(3 * k + b, 1), :]
-                    high, low = split(m)
-                    m_hi[n, to, p * CW : (p + 1) * CW] = high
-                    m_lo[n, to, p * CW : (p + 1) * CW] = low
-            return c
-
-        lax.fori_loop(0, 9, column_ops, 0)
+    pltpu.make_async_copy(msend.at[my_plane], mrelay.at[my_plane], msem.at[0]).start()
+
+    def relay_meta():
+        pltpu.make_async_copy(msend, mrelay, msem.at[0]).wait()
+        for k in range(1, GROUP):
+            place = lax.rem(mine + k, GROUP)
+            pltpu.make_async_remote_copy(
+                src_ref=mrelay.at[:, place],
+                dst_ref=mrecv.at[:, mine],
+                send_sem=send_sem.at[2],
+                recv_sem=msem.at[1],
+                device_id=(my_plane * GROUP + place, band),
+                device_id_type=MESH,
+            ).start()
+        pltpu.make_async_copy(mrelay.at[:, mine], mrecv.at[:, mine], msem.at[1]).start()
+
+    if flux_mode:
         y = 2.0 * lax.broadcasted_iota(jnp.int32, (CH, 1), 0).astype(F32) / (CH - 1) - 1.0
         for n in range(CCDS):
             o = dot(s_hi[n], m_hi[n]) + dot(s_hi[n], m_lo[n]) + dot(s_lo[n], m_hi[n])
             conv = o[:, :CW] + y * o[:, CW : 2 * CW] + (y * y) * o[:, 2 * CW :]
-            at = pl.ds(n * CH, CH)
-            use[at, :] = use[at, :] * conv
-    else:
-
-        def meta_step(k, c):
-            send_meta(k)
-            return c
-
-        lax.fori_loop(1, DEVS, meta_step, 0)
+            for k in range(CH // SR):
+                at = pl.ds(n * CH + k * SR, SR)
+                flux = use[at, :] * conv[k * SR : (k + 1) * SR, :]
+                tmp[at, :] = pltpu.roll(
+                    flux, lax.bitwise_and(col_s[0, n * (CH // SR) + k], CW - 1), 1
+                )
 
     def roll_strip(s, c):
         at = pl.ds(pl.multiple_of(s * SR, SR), SR)
         tmp[at, :] = pltpu.roll(use[at, :], lax.bitwise_and(col_s[0, s], CW - 1), 1)
         return c
 
-    lax.fori_loop(0, STRIPS, roll_strip, 0, unroll=8)
+    if not flux_mode:
+        lax.fori_loop(0, STRIPS, roll_strip, 0, unroll=8)
     for i in range(SR):
         high, low = split(tmp[pl.ds(i, STRIPS, stride=SR), :])
         packed[pl.ds(i, DEVS * SLOTS, stride=SR), :] = dot(hot[...], high) + dot(hot[...], low)
@@ -288,6 +301,7 @@
         lax.fori_loop(0, DEVS // 2, one, 0)
 
     send_half(0)
+    relay_meta()
     send_half(1)
     pltpu.make_async_copy(
         packed.at[block(me)], arrived.at[block(me)], data_sem.at[my_plane]
@@ -313,7 +327,6 @@
             pltpu.make_async_copy(rest, rest, flag_sem.at[k, r]).wait()
         return jnp.max(land[...].reshape(n + 1, CW), axis=0, keepdims=True)
 
-    mine = lax.rem(me, GROUP)
     if flux_mode:
         nonzero = jnp.sum(jnp.where(packed[...] != 0.0, 1.0, 0.0))
         flag = jnp.zeros((1, CW), F32) + (usable_count - nonzero)
@@ -322,16 +335,7 @@
             [(my_plane * GROUP + lax.rem(mine + k, GROUP), band) for k in range(1, GROUP)],
         )
 
-    own_meta.wait()
-    all_meta = pltpu.make_async_remote_copy(
-        src_ref=msend.at[pl.ds(0, DEVS - 1)],
-        dst_ref=mrecv.at[pl.ds(0, DEVS - 1)],
-        send_sem=send_sem.at[1],
-        recv_sem=msem,
-        device_id=(me, band),
-        device_id_type=MESH,
-    )
-    all_meta.wait_recv()
+    pltpu.make_async_copy(mrelay, mrecv, msem.at[1]).wait()
     if flux_mode:
         flag_round(
             1, flag_end(0, flag_plane), flag_z, my_plane,
@@ -410,7 +414,9 @@
     else:
         wgt_o[...] = placed[...]
 
-    all_meta.wait_send()
+    for k in (1, 2):
+        others = mrelay.at[pl.ds(0, PLANES - 1)]
+        pltpu.make_async_copy(others, others, send_sem.at[k]).wait()
     rest = packed.at[pl.ds(0, (DEVS - 1) * BLOCK)]
     pltpu.make_async_copy(rest, rest, send_sem.at[0]).wait()
 
@@ -452,9 +458,10 @@
             pltpu.VMEM((CCDS, 3, NB, CW), F32),
             pltpu.VMEM((DEVS * SLOTS, STRIPS), BF16),
             pltpu.VMEM((slots, CW), F32),
-            pltpu.VMEM((DEVS, 1, CW), F32),
+            pltpu.VMEM((PLANES, GROUP, 1, CW), F32),
+            pltpu.VMEM((PLANES, GROUP, 1, CW), F32),
             pltpu.VMEM((slots, CW), F32),
-            pltpu.VMEM((DEVS, 1, CW), F32),
+            pltpu.VMEM((PLANES, GROUP, 1, CW), F32),
             pltpu.VMEM((slots, CW), F32),
             pltpu.VMEM((slots, CW), F32),
             pltpu.VMEM((PLANES, PH, 2 * CHUNK), BF16),
@@ -465,10 +472,10 @@
             pltpu.VMEM((GROUP, 1, CW), F32),
             pltpu.VMEM((PLANES, 1, CW), F32),
             pltpu.VMEM((BANDS, 1, CW), F32),
-            pltpu.SemaphoreType.DMA((13,)),
+            pltpu.SemaphoreType.DMA((12,)),
+            pltpu.SemaphoreType.DMA((3,)),
+            pltpu.SemaphoreType.DMA((PLANES,)),
             pltpu.SemaphoreType.DMA((2,)),
-            pltpu.SemaphoreType.DMA((PLANES,)),
-            pltpu.SemaphoreType.DMA,
             pltpu.SemaphoreType.DMA((2, 3)),
         ],
         compiler_params=pltpu.CompilerParams(

time: 35.9 us -> 33.4 us (0.930)
  Pallas kernels: 34.3 us -> 31.8 us
    pallas_call x1, Pallas kernels: 34.3 us -> 31.8 us  [exchange(): pl.pallas_call(functools.partial(kernel, flux_mode), out_shape=outs, in_s...]
where the time goes in v4:
time: 33.4 us; the launch traced here: 33.3 us
  Pallas kernels  31.8 us (95%)
  other arithmetic  0.82 us (2%)
  between operations  0.68 us (2%)
    pallas_call x1, Pallas kernels, exchange(): pl.pallas_call(functools.partial(kernel, flux_mode), out_shape=outs, in_s...  31.8 us
    broadcast_in_dim x1, other arithmetic, finish(): return ((num / jnp.maximum(wgt, 1.0))[None], jnp.maximum(wgt, 0.0)[None])  0.82 us

profile of v4, /device:TPU:1, one launch (start us, length us, event | category | flops | bytes accessed | tf_op | source)
XLA Modules:
  0.0 33.3 jit_solution(14828489253305492182)
XLA Ops:
  0.6 31.8 %shard_map.122 = (f32[128,512]{1,0:T(8,128)S(1)}, f32[128,512]{1,0:T(8,128)S(1)}, f32[1,128]{1,0:T(1,128)S(1)}) custom-call(s32[512,128]{1,0:T(8,128)} %bitcast.15, f32[512,128]{1,0:T(8,128)} %bitcast.17, f32[512,128]{1,0:T(8,128)} %bitcast.19, f32[6,2,27]{2,1,0:T(2,128)} %bitcast.21, s32[1,2]{1,0:T(1,128)} %bitcast.23, s32[1,64]{1,0:T(1,128)} %bitcast.25, ...), custom_call_target="tpu_custom_call" | custom-call | flops 2600000000 | bytes 6000000 | tf_op jit(solution)/shard_map/pallas_call | solution.py:432
  32.5 0.8 %maximum_bitcast_fusion = (f32[1,128,512]{2,1,0:T(8,128)}, f32[1,128,512]{2,1,0:T(8,128)}) fusion(f32[128,512]{1,0:T(8,128)S(1)} %get-tuple-element.51, f32[128,512]{1,0:T(8,128)S(1)} %get-tuple-element.50), kind=kLoop, calls=%fused_computation.1 | loop fusion | flops 196608 | bytes 1048576 | tf_op jit(solution)/shard_map/cond/branch_0_fun/broadcast_in_dim | solution.py:513
  (1 shorter events, 0.0 us)

commit v5 on v4

--- a/solution.py
+++ b/solution.py
@@ -60,6 +60,19 @@
 def split(x):
     high = x.astype(BF16)
     return high, (x - high.astype(F32)).astype(BF16)
+
+
+def halves(x):
+    scaled = x * 4097.0
+    high = scaled - (scaled - x)
+    return high, x - high
+
+
+def product(a, b):
+    p = a * b
+    a_high, a_low = halves(a)
+    b_high, b_low = halves(b)
+    return p, ((a_high * b_high - p) + a_high * b_low + a_low * b_high) + a_low * b_low
 
 
 def dot(a, b):
@@ -259,7 +272,9 @@
         y = 2.0 * lax.broadcasted_iota(jnp.int32, (CH, 1), 0).astype(F32) / (CH - 1) - 1.0
         for n in range(CCDS):
             o = dot(s_hi[n], m_hi[n]) + dot(s_hi[n], m_lo[n]) + dot(s_lo[n], m_hi[n])
-            conv = o[:, :CW] + y * o[:, CW : 2 * CW] + (y * y) * o[:, 2 * CW :]
+            first, first_rest = product(y, o[:, CW : 2 * CW])
+            second, second_rest = product(y * y, o[:, 2 * CW :])
+            conv = (o[:, :CW] + first + second) + (first_rest + second_rest)
             for k in range(CH // SR):
                 at = pl.ds(n * CH + k * SR, SR)
                 flux = use[at, :] * conv[k * SR : (k + 1) * SR, :]

time: 33.4 us -> 33.5 us (level)
  no operation moved by 1% of the time
where the time goes in v5:
time: 33.5 us; the launch traced here: 33.4 us
  Pallas kernels  31.9 us (95%)
  other arithmetic  0.82 us (2%)
  between operations  0.68 us (2%)
    pallas_call x1, Pallas kernels, exchange(): pl.pallas_call(functools.partial(kernel, flux_mode), out_shape=outs, in_s...  31.9 us
    broadcast_in_dim x1, other arithmetic, finish(): return ((num / jnp.maximum(wgt, 1.0))[None], jnp.maximum(wgt, 0.0)[None])  0.82 us

profile of v5, /device:TPU:1, one launch (start us, length us, event | category | flops | bytes accessed | tf_op | source)
XLA Modules:
  0.0 33.4 jit_solution(10131259278836322017)
XLA Ops:
  0.6 31.9 %shard_map.122 = (f32[128,512]{1,0:T(8,128)S(1)}, f32[128,512]{1,0:T(8,128)S(1)}, f32[1,128]{1,0:T(1,128)S(1)}) custom-call(s32[512,128]{1,0:T(8,128)} %bitcast.15, f32[512,128]{1,0:T(8,128)} %bitcast.17, f32[512,128]{1,0:T(8,128)} %bitcast.19, f32[6,2,27]{2,1,0:T(2,128)} %bitcast.21, s32[1,2]{1,0:T(1,128)} %bitcast.23, s32[1,64]{1,0:T(1,128)} %bitcast.25, ...), custom_call_target="tpu_custom_call" | custom-call | flops 2600000000 | bytes 6000000 | tf_op jit(solution)/shard_map/pallas_call | solution.py:447
  32.6 0.8 %maximum_bitcast_fusion = (f32[1,128,512]{2,1,0:T(8,128)}, f32[1,128,512]{2,1,0:T(8,128)}) fusion(f32[128,512]{1,0:T(8,128)S(1)} %get-tuple-element.51, f32[128,512]{1,0:T(8,128)S(1)} %get-tuple-element.50), kind=kLoop, calls=%fused_computation.1 | loop fusion | flops 196608 | bytes 1048576 | tf_op jit(solution)/shard_map/cond/branch_0_fun/broadcast_in_dim | solution.py:528
  (1 shorter events, 0.0 us)

commit v6 on v5

--- a/solution.py
+++ b/solution.py
@@ -239,6 +239,30 @@
         for k in range(9):
             row_pass(k, 0)
 
+    def columns_and_pack():
+        y = 2.0 * lax.broadcasted_iota(jnp.int32, (CH, 1), 0).astype(F32) / (CH - 1) - 1.0
+        for n in range(CCDS):
+            o = dot(s_hi[n], m_hi[n]) + dot(s_hi[n], m_lo[n]) + dot(s_lo[n], m_hi[n])
+            first, first_rest = product(y, o[:, CW : 2 * CW])
+            second, second_rest = product(y * y, o[:, 2 * CW :])
+            conv = (o[:, :CW] + first + second) + (first_rest + second_rest)
+            for k in range(CH // SR):
+                at = pl.ds(n * CH + k * SR, SR)
+                flux = use[at, :] * conv[k * SR : (k + 1) * SR, :]
+                tmp[at, :] = pltpu.roll(
+                    flux, lax.bitwise_and(col_s[0, n * (CH // SR) + k], CW - 1), 1
+                )
+        for i in range(SR):
+            high, low = split(tmp[pl.ds(i, STRIPS, stride=SR), :])
+            packed[pl.ds(i, DEVS * SLOTS, stride=SR), :] = dot(hot[...], high) + dot(hot[...], low)
+
+    early = me < DEVS // 2
+    if flux_mode:
+
+        @pl.when(early)
+        def _():
+            columns_and_pack()
+
     pl.semaphore_wait(barrier, greeted)
 
     mine = lax.rem(me, GROUP)
@@ -269,29 +293,21 @@
         pltpu.make_async_copy(mrelay.at[:, mine], mrecv.at[:, mine], msem.at[1]).start()
 
     if flux_mode:
-        y = 2.0 * lax.broadcasted_iota(jnp.int32, (CH, 1), 0).astype(F32) / (CH - 1) - 1.0
-        for n in range(CCDS):
-            o = dot(s_hi[n], m_hi[n]) + dot(s_hi[n], m_lo[n]) + dot(s_lo[n], m_hi[n])
-            first, first_rest = product(y, o[:, CW : 2 * CW])
-            second, second_rest = product(y * y, o[:, 2 * CW :])
-            conv = (o[:, :CW] + first + second) + (first_rest + second_rest)
-            for k in range(CH // SR):
-                at = pl.ds(n * CH + k * SR, SR)
-                flux = use[at, :] * conv[k * SR : (k + 1) * SR, :]
-                tmp[at, :] = pltpu.roll(
-                    flux, lax.bitwise_and(col_s[0, n * (CH // SR) + k], CW - 1), 1
-                )
-
-    def roll_strip(s, c):
-        at = pl.ds(pl.multiple_of(s * SR, SR), SR)
-        tmp[at, :] = pltpu.roll(use[at, :], lax.bitwise_and(col_s[0, s], CW - 1), 1)
-        return c
-
-    if not flux_mode:
+
+        @pl.when(jnp.logical_not(early))
+        def _():
+            columns_and_pack()
+
+    else:
+        def roll_strip(s, c):
+            at = pl.ds(pl.multiple_of(s * SR, SR), SR)
+            tmp[at, :] = pltpu.roll(use[at, :], lax.bitwise_and(col_s[0, s], CW - 1), 1)
+            return c
+
         lax.fori_loop(0, STRIPS, roll_strip, 0, unroll=8)
-    for i in range(SR):
-        high, low = split(tmp[pl.ds(i, STRIPS, stride=SR), :])
-        packed[pl.ds(i, DEVS * SLOTS, stride=SR), :] = dot(hot[...], high) + dot(hot[...], low)
+        for i in range(SR):
+            high, low = split(tmp[pl.ds(i, STRIPS, stride=SR), :])
+            packed[pl.ds(i, DEVS * SLOTS, stride=SR), :] = dot(hot[...], high) + dot(hot[...], low)
 
     def block(d):
         return pl.ds(pl.multiple_of(d * BLOCK, BLOCK), BLOCK)

time: 33.5 us -> 32.7 us (0.976); the launches traced: 33.4 us -> 32.2 us
  Pallas kernels: 31.9 us -> 30.7 us
    pallas_call x1, Pallas kernels: 31.9 us -> 30.7 us  [exchange(): pl.pallas_call(functools.partial(kernel, flux_mode), out_shape=outs, in_s...]
where the time goes in v6:
time: 32.7 us; the launch traced here: 32.2 us
  Pallas kernels  30.7 us (94%)
  other arithmetic  0.82 us (3%)
  between operations  0.68 us (2%)
    pallas_call x1, Pallas kernels, exchange(): pl.pallas_call(functools.partial(kernel, flux_mode), out_shape=outs, in_s...  30.7 us
    broadcast_in_dim x1, other arithmetic, finish(): return ((num / jnp.maximum(wgt, 1.0))[None], jnp.maximum(wgt, 0.0)[None])  0.82 us

profile of v6, /device:TPU:1, one launch (start us, length us, event | category | flops | bytes accessed | tf_op | source)
XLA Modules:
  0.0 32.2 jit_solution(4452404341494603649)
XLA Ops:
  0.6 30.7 %shard_map.122 = (f32[128,512]{1,0:T(8,128)S(1)}, f32[128,512]{1,0:T(8,128)S(1)}, f32[1,128]{1,0:T(1,128)S(1)}) custom-call(s32[512,128]{1,0:T(8,128)} %bitcast.15, f32[512,128]{1,0:T(8,128)} %bitcast.17, f32[512,128]{1,0:T(8,128)} %bitcast.19, f32[6,2,27]{2,1,0:T(2,128)} %bitcast.21, s32[1,2]{1,0:T(1,128)} %bitcast.23, s32[1,64]{1,0:T(1,128)} %bitcast.25, ...), custom_call_target="tpu_custom_call" | custom-call | flops 2600000000 | bytes 6000000 | tf_op jit(solution)/shard_map/pallas_call | solution.py:463
  31.4 0.8 %maximum_bitcast_fusion = (f32[1,128,512]{2,1,0:T(8,128)}, f32[1,128,512]{2,1,0:T(8,128)}) fusion(f32[128,512]{1,0:T(8,128)S(1)} %get-tuple-element.51, f32[128,512]{1,0:T(8,128)S(1)} %get-tuple-element.50), kind=kLoop, calls=%fused_computation.1 | loop fusion | flops 196608 | bytes 1048576 | tf_op jit(solution)/shard_map/cond/branch_0_fun/broadcast_in_dim | solution.py:544
  (1 shorter events, 0.0 us)

commit v7 on v6

--- a/solution.py
+++ b/solution.py
@@ -417,27 +417,35 @@
 
     placed[...] = jnp.zeros_like(placed)
 
-    def place(p, c):
-        at = pl.ds(pl.multiple_of(p * CHUNK, CHUNK), CHUNK)
-        pltpu.make_async_copy(packed.at[at], arrived.at[at], data_sem.at[p]).wait()
-        value = arrived[at, :]
-        weight = vrep[at, :]
-        maps = [value * weight]
-        if flux_mode:
-            maps.append(jnp.where(value != 0.0, weight, 0.0))
-        off = crep[at, :]
-        for n, (high, low) in enumerate(split(m) for m in maps):
-            zero = jnp.zeros_like(high)
-            for t in range(PW // CW):
-                away = off + float(t * CW)
-                inside = (away >= 0.0) & (away < CW)
-                cols = pl.ds(n * PW + t * CW, CW)
-                wide[0:CHUNK, cols] = jnp.where(inside, high, zero)
-                wide[CHUNK : 2 * CHUNK, cols] = jnp.where(inside, low, zero)
-        placed[...] += dot(rows_of[p], wide[...])
+    def place(pair, c):
+        total = 0.0
+        for m in range(2):
+            at = pl.ds(pl.multiple_of((2 * pair + m) * CHUNK, CHUNK), CHUNK)
+            pltpu.make_async_copy(
+                packed.at[at], arrived.at[at], data_sem.at[2 * pair + m]
+            ).wait()
+        for m in range(2):
+            p = 2 * pair + m
+            at = pl.ds(pl.multiple_of(p * CHUNK, CHUNK), CHUNK)
+            value = arrived[at, :]
+            weight = vrep[at, :]
+            maps = [value * weight]
+            if flux_mode:
+                maps.append(jnp.where(value != 0.0, weight, 0.0))
+            off = crep[at, :]
+            for n, (high, low) in enumerate(split(v) for v in maps):
+                zero = jnp.zeros_like(high)
+                for t in range(PW // CW):
+                    away = off + float(t * CW)
+                    inside = (away >= 0.0) & (away < CW)
+                    cols = pl.ds(n * PW + t * CW, CW)
+                    wide[m, 0:CHUNK, cols] = jnp.where(inside, high, zero)
+                    wide[m, CHUNK : 2 * CHUNK, cols] = jnp.where(inside, low, zero)
+            total = total + dot(rows_of[p], wide[m])
+        placed[...] += total
         return c
 
-    lax.fori_loop(0, PLANES, place, 0)
+    lax.fori_loop(0, PLANES // 2, place, 0)
     if flux_mode:
         num_o[...] = placed[:, :PW]
         wgt_o[...] = placed[:, PW:]
@@ -496,7 +504,7 @@
             pltpu.VMEM((slots, CW), F32),
             pltpu.VMEM((slots, CW), F32),
             pltpu.VMEM((PLANES, PH, 2 * CHUNK), BF16),
-            pltpu.VMEM((2 * CHUNK, maps * PW), BF16),
+            pltpu.VMEM((2, 2 * CHUNK, maps * PW), BF16),
             pltpu.VMEM((SLOTS * DEVS, 3 * CW), F32),
             pltpu.VMEM((PH, maps * PW), F32),
             pltpu.VMEM((3, 1, CW), F32),

time: 32.7 us -> 32.7 us (level)
  no operation moved by 1% of the time
where the time goes in v7:
time: 32.7 us; the launch traced here: 32.2 us
  Pallas kernels  30.7 us (94%)
  other arithmetic  0.82 us (3%)
  between operations  0.68 us (2%)
    pallas_call x1, Pallas kernels, exchange(): pl.pallas_call(functools.partial(kernel, flux_mode), out_shape=outs, in_s...  30.7 us
    broadcast_in_dim x1, other arithmetic, finish(): return ((num / jnp.maximum(wgt, 1.0))[None], jnp.maximum(wgt, 0.0)[None])  0.82 us

profile of v7, /device:TPU:1, one launch (start us, length us, event | category | flops | bytes accessed | tf_op | source)
XLA Modules:
  0.0 32.2 jit_solution(7645818765735331504)
XLA Ops:
  0.6 30.7 %shard_map.122 = (f32[128,512]{1,0:T(8,128)S(1)}, f32[128,512]{1,0:T(8,128)S(1)}, f32[1,128]{1,0:T(1,128)S(1)}) custom-call(s32[512,128]{1,0:T(8,128)} %bitcast.15, f32[512,128]{1,0:T(8,128)} %bitcast.17, f32[512,128]{1,0:T(8,128)} %bitcast.19, f32[6,2,27]{2,1,0:T(2,128)} %bitcast.21, s32[1,2]{1,0:T(1,128)} %bitcast.23, s32[1,64]{1,0:T(1,128)} %bitcast.25, ...), custom_call_target="tpu_custom_call" | custom-call | flops 2600000000 | bytes 6000000 | tf_op jit(solution)/shard_map/pallas_call | solution.py:471
  31.4 0.8 %maximum_bitcast_fusion = (f32[1,128,512]{2,1,0:T(8,128)}, f32[1,128,512]{2,1,0:T(8,128)}) fusion(f32[128,512]{1,0:T(8,128)S(1)} %get-tuple-element.51, f32[128,512]{1,0:T(8,128)S(1)} %get-tuple-element.50), kind=kLoop, calls=%fused_computation.1 | loop fusion | flops 196608 | bytes 1048576 | tf_op jit(solution)/shard_map/cond/branch_0_fun/broadcast_in_dim | solution.py:552
  (1 shorter events, 0.0 us)
